TPU v7x, 128 devices: a whole 4x4x4 slice. The times are simulated.
128 devices in a mesh: seq: 16 (over y_hi, x, core), tp: 8 (over y_lo, z).
Axes of the slice: x: 4, y: 4 (y_hi: 2, y_lo: 2; y = y_hi * 2 + y_lo), z: 4, core: 2. Of those that a mesh axis runs over, the one named last changes fastest.
Arguments:
- hidden: bfloat16 [8192, 2560], P('seq', 'tp'), may hold values from -6 to 6
- norm_gain: float32 [2560], replicated, may hold values from 0.25 to 1.75
- query_weight: float32 [2560, 4096], P('seq', 'tp'), may hold values from -0.125 to 0.125
- key_weight: float32 [2560, 1024], P('seq', 'tp'), may hold values from -0.125 to 0.125
- value_weight: float32 [2560, 1024], P('seq', 'tp'), may hold values from -0.125 to 0.125
- query_gain: float32 [128], replicated, may hold values from 0.5 to 8
- key_gain: float32 [128], replicated, may hold values from 0.5 to 8
- lengths: int32 [8], replicated, may hold values from 1 to 4096, 8192 in all
- page_table: int32 [64], replicated, may hold values from 0 to 63, each once
Outputs:
- attention: bfloat16 [8192, 4096], P('seq', 'tp')
- key_cache: bfloat16 [64, 8, 128, 128], P('seq', 'tp')
- value_cache: bfloat16 [64, 8, 128, 128], P('seq', 'tp')
Inputs may be any that keep to these rules, and one draw needn't show every extreme that they name: 8 positive lengths summing to 8192; the longest is exactly 4096. `page_table`: every page is named by exactly one block.
All inputs are finite; a program needn't handle non-finite values.
Results may differ from a plain program's by a relative error of at most 0.0085.
The roundings to bfloat16 on the way count: a program that leaves them out, or rounds other values in their place, can miss the bound.
Values may be sent and summed in bfloat16 or wider, within the bound.
A program may use at most 128 MiB of HBM per device.

v0:
```python
from functools import partial

import jax
import jax.numpy as jnp
from jax import lax
from jax.sharding import PartitionSpec as P

PAGE = 128


epsilon = 1e-06
excluded = -1e30


def segment_of(slot_index, prompt_ends):
    return jnp.sum((slot_index[..., None] >= prompt_ends).astype(jnp.int32), axis=-1)


def position_of(slot_index, prompt_ends, lengths):
    segment_id = segment_of(slot_index, prompt_ends)
    prompt_starts = prompt_ends - lengths
    labels = jnp.arange(lengths.shape[0], dtype=jnp.int32)
    picked = jnp.sum(jnp.where(segment_id[..., None] == labels, prompt_starts, 0), axis=-1)
    return (segment_id, slot_index - picked)


def head_norm(vectors, gain):
    mean_sq = jnp.mean(vectors * vectors, axis=-1, keepdims=True)
    return vectors * lax.rsqrt(mean_sq + epsilon) * gain


def rotate(vectors, position):
    head_dim = vectors.shape[-1]
    half_dim = head_dim // 2
    frequency = 1000000.0 ** (-(jnp.arange(half_dim, dtype=jnp.float32) * 2.0 / head_dim))
    angles = position.astype(jnp.float32)[:, None] * frequency[None, :]
    cosine = jnp.cos(angles)[:, None, :]
    sine_part = jnp.sin(angles)[:, None, :]
    front = vectors[..., :half_dim]
    back_half = vectors[..., half_dim:]
    return jnp.concatenate(
        [front * cosine - back_half * sine_part, back_half * cosine + front * sine_part], axis=-1
    )


def attend(
    query_block,
    query_slots,
    query_segments,
    key_piece,
    value_piece,
    key_slots,
    key_segments,
    kv_heads,
    group_size,
    head_dim,
    running,
):
    running_max, denominator, accumulator = running
    half_rows = query_block.shape[0]
    key_count = key_piece.shape[0]
    scores = jnp.einsum(
        "qkgd,nkd->kgqn",
        query_block.reshape(half_rows, kv_heads, group_size, head_dim),
        key_piece.reshape(key_count, kv_heads, head_dim),
        preferred_element_type=jnp.float32,
    ) * head_dim ** (-0.5)
    allowed = (key_segments[None, :] == query_segments[:, None]) & (
        key_slots[None, :] <= query_slots[:, None]
    )
    masked = jnp.where(allowed, scores, excluded)
    new_max = jnp.maximum(running_max, jnp.max(masked, axis=-1))
    weights = jnp.where(allowed, jnp.exp(scores - new_max[..., None]), 0.0)
    denominator = jnp.sum(weights, axis=-1)
    probs = weights.astype(jnp.bfloat16)
    accumulator = jnp.einsum(
        "kgqn,nkd->kgqd",
        probs,
        value_piece.reshape(key_count, kv_heads, head_dim),
        preferred_element_type=jnp.float32,
    )
    return (new_max, denominator, accumulator)


def keep_state(running):
    return running


def shards(
    hidden,
    norm_gain,
    query_weight,
    key_weight,
    value_weight,
    query_gain,
    key_gain,
    lengths,
    page_table,
):
    row_count = hidden.shape[0]
    half_rows = row_count // 2
    head_dim = query_gain.shape[0]
    query_cols = query_weight.shape[1]
    key_cols = key_weight.shape[1]
    kv_heads = key_cols // head_dim
    group_size = query_cols // key_cols
    seq_rank = lax.axis_index("seq")
    prompt_ends = jnp.cumsum(lengths)
    gathered = lax.all_gather(hidden, "tp", axis=1, tiled=True)
    widened = gathered.astype(jnp.float32)
    normed = (
        widened
        * lax.rsqrt(jnp.mean(widened * widened, axis=-1, keepdims=True) + epsilon)
        * norm_gain
    ).astype(jnp.bfloat16)
    server_block = jnp.concatenate([query_weight, key_weight, value_weight], axis=1).astype(
        jnp.bfloat16
    )
    projected = jnp.dot(
        normed,
        lax.all_gather(server_block, "seq", axis=0, tiled=True),
        preferred_element_type=jnp.float32,
    )
    slot_index = seq_rank * row_count + jnp.arange(row_count, dtype=jnp.int32)
    segment_id, position = position_of(slot_index, prompt_ends, lengths)
    queries = rotate(
        head_norm(
            projected[:, :query_cols].reshape(row_count, query_cols // head_dim, head_dim),
            query_gain,
        ),
        position,
    )
    queries = queries.reshape(row_count, query_cols).astype(jnp.bfloat16)
    key_rows = rotate(
        head_norm(
            projected[:, query_cols : query_cols + key_cols].reshape(row_count, kv_heads, head_dim),
            key_gain,
        ),
        position,
    )
    key_rows = key_rows.reshape(row_count, key_cols).astype(jnp.bfloat16)
    values = projected[:, query_cols + key_cols :].astype(jnp.bfloat16)
    shipped = queries[half_rows:]
    other_slots = slot_index[half_rows:]
    query_blocks = (queries[:half_rows], shipped)
    block_slots = (slot_index[:half_rows], other_slots)
    block_segments = (
        segment_of(block_slots[0], prompt_ends),
        segment_of(block_slots[1], prompt_ends),
    )
    pages_dev = row_count // PAGE
    owned_pages = seq_rank * pages_dev + jnp.arange(pages_dev, dtype=jnp.int32)
    page_count = page_table.shape[0]
    source_block = jnp.sum(
        jnp.where(
            page_table[None, :] == owned_pages[:, None],
            jnp.arange(page_count, dtype=jnp.int32)[None, :],
            0,
        ),
        axis=1,
    )

    def empty_state():
        return (
            jnp.full((kv_heads, group_size, half_rows), excluded, jnp.float32),
            jnp.zeros((kv_heads, group_size, half_rows), jnp.float32),
            jnp.zeros((kv_heads, group_size, half_rows, head_dim), jnp.float32),
        )

    empty_pages = jnp.zeros((pages_dev, PAGE, key_cols), jnp.bfloat16)
    initial = (empty_state(), empty_state(), empty_pages, empty_pages)
    first_row = jnp.int32(0)
    key_piece = lax.all_gather(key_rows, "seq", axis=0, tiled=True)
    value_piece = lax.all_gather(values, "seq", axis=0, tiled=True)
    key_count = key_piece.shape[0]
    key_slots = jnp.arange(key_count, dtype=jnp.int32)
    key_segments = segment_of(key_slots, prompt_ends)
    states = []
    for fold_half_number in range(2):
        query_slots = block_slots[fold_half_number]
        query_segments = block_segments[fold_half_number]
        last_query = query_slots[-1]
        clipped = jnp.minimum(first_row + key_count - 1, last_query)
        is_live = (first_row <= last_query) & (
            segment_of(clipped, prompt_ends) >= query_segments[0]
        )
        update = partial(
            attend,
            query_blocks[fold_half_number],
            query_slots,
            query_segments,
            key_piece,
            value_piece,
            key_slots,
            key_segments,
            kv_heads,
            group_size,
            head_dim,
        )
        states.append(lax.cond(is_live, update, keep_state, initial[fold_half_number]))
    blocks_in = key_count // PAGE
    block_number = jnp.arange(blocks_in, dtype=jnp.int32)
    matches = source_block[:, None] == block_number[None, :]
    selector = matches.astype(jnp.bfloat16)
    has_page = jnp.any(matches, axis=1)[:, None, None]
    new_keys = jnp.einsum(
        "pj,jtc->ptc",
        selector,
        key_piece.reshape(blocks_in, PAGE, key_cols),
        preferred_element_type=jnp.float32,
    ).astype(jnp.bfloat16)
    new_values = jnp.einsum(
        "pj,jtc->ptc",
        selector,
        value_piece.reshape(blocks_in, PAGE, key_cols),
        preferred_element_type=jnp.float32,
    ).astype(jnp.bfloat16)
    key_pages = jnp.where(has_page, new_keys, initial[2])
    value_pages = jnp.where(has_page, new_values, initial[3])
    result = (states[0], states[1], key_pages, value_pages)
    outputs = []
    for half_number in range(2):
        running_max, denominator, accumulator = result[half_number]
        result_block = accumulator / denominator[..., None]
        outputs.append(
            result_block.transpose(2, 0, 1, 3).reshape(half_rows, query_cols).astype(jnp.bfloat16)
        )
    returned = outputs[1]
    attention = jnp.concatenate([outputs[0], returned], axis=0)
    key_cache = result[2].reshape(pages_dev, PAGE, kv_heads, head_dim).transpose(0, 2, 1, 3)
    value_cache = result[3].reshape(pages_dev, PAGE, kv_heads, head_dim).transpose(0, 2, 1, 3)
    return (attention, key_cache, value_cache)


def solution(mesh):
    return jax.shard_map(
        shards,
        mesh=mesh,
        in_specs=(
            P("seq", "tp"),
            P(),
            P("seq", "tp"),
            P("seq", "tp"),
            P("seq", "tp"),
            P(),
            P(),
            P(),
            P(),
        ),
        out_specs=(P("seq", "tp"), P("seq", "tp", None, None), P("seq", "tp", None, None)),
        check_vma=False,
    )
```

profile of v0, /device:TPU:24, one launch (start us, length us, event | category | flops | bytes accessed | tf_op | source)
XLA Modules:
  0.0 336.8 jit_solution(13520177718154089002)
XLA Ops:
  7.2 0.0 all-gather.6.cloned.1.call-start
  7.2 0.7 all-gather.6.cloned.1.call-update
  7.9 0.0 all-gather.8.cloned.1.call-start
  7.9 1.0 convert.24
  8.9 0.9 convert.25
  9.8 0.9 convert.26
  10.7 0.7 pad_maximum_fusion.2
  11.4 0.0 all-gather.8.cloned.1.call-update
  11.5 0.0 all-gather.12.cloned.1.call-start
  11.5 0.6 fusion.77
  13.4 0.8 reduce-window.8
  14.2 0.1 convert_reduce_fusion.1
  14.3 1.4 fusion.74
  15.7 0.1 select_reduce_fusion
  15.7 37.8 %all-gather.6.cloned.1.call-done = bf16[512,2560]{0,1:T(8,128)(2,1)} async-done(((bf16[512,320]{0,1:T(8,128)(2,1)}), bf16[512,2560]{0,1:T(8,128)(2,1)}) %all-gather.6.cloned.1.call-update) | async-done | bytes 2621456 | tf_op jit(solution)/shard_map/all_gather | solution.py:109
  53.6 2.4 fusion.38
  56.0 54.0 %all-gather.8.cloned.1.call-done = bf16[2560,768]{1,0:T(8,128)(2,1)} async-done(((bf16[160,768]{1,0:T(8,128)(2,1)}), bf16[2560,768]{1,0:T(8,128)(2,1)}) %all-gather.8.cloned.1.call-update) | async-done | bytes 3932176 | tf_op jit(solution)/shard_map/all_gather | solution.py:121
  110.0 5.4 %fusion.41 = f32[512,768]{1,0:T(8,128)S(1)} fusion(bf16[2560,768]{1,0:T(8,128)(2,1)} %all-gather.8.cloned.1.call-done, bf16[512,2560]{0,1:T(8,128)(2,1)} %all-gather.6.cloned.1.call-done, f32[2560]{0:T(1024)} %param.14, f32[512]{0:T(512)S(1)} %add_rsqrt_fusion.2), kind=kOutput, calls=%fused_computation.41 | convolution fusion | flops 2018508800 | bytes 8138752 | tf_op jit(solution)/shard_map/dot_general | solution.py:119
  115.4 0.1 copy.81
  115.6 0.1 multiply_bitcast_fusion
  115.7 0.6 fusion.65
  116.3 0.7 pad_maximum_fusion.3
  116.9 0.0 all-gather.12.cloned.1.call-update
  117.0 0.0 all-gather.10.cloned.1.call-start
  117.0 0.7 slice.79
  117.7 0.0 all-gather.10.cloned.1.call-update
  118.9 0.1 convert_reduce_fusion.3
  119.0 0.6 slice.52
  120.9 0.5 slice.62
  122.7 0.2 select_reduce_fusion.1
  122.9 0.2 fusion.69
  123.1 0.1 convert_reduce_fusion
  123.2 1.0 multiply_cosine_fusion
  124.2 1.3 slice.63
  125.5 0.4 reshape.285
  125.9 0.6 multiply_reduce_fusion
  126.6 0.7 multiply_multiply_fusion
  127.3 0.8 subtract_convert_fusion
  128.1 0.7 pad_maximum_fusion
  128.8 0.3 copy.63
  129.2 36.3 %all-gather.12.cloned.1.call-done = bf16[8192,1,128]{0,2,1:T(8,128)(2,1)} async-done(((bf16[512,1,128]{0,2,1:T(8,128)(2,1)}), bf16[8192,1,128]{0,2,1:T(8,128)(2,1)}) %all-gather.12.cloned.1.call-update) | async-done | bytes 2097168 | tf_op jit(solution)/shard_map/all_gather | solution.py:173
  165.4 50.0 %all-gather.10.cloned.1.call-done = bf16[8192,128]{1,0:T(8,128)(2,1)} async-done(((bf16[512,128]{1,0:T(8,128)(2,1)}), bf16[8192,128]{1,0:T(8,128)(2,1)}) %all-gather.10.cloned.1.call-update) | async-done | bytes 2097168 | tf_op jit(solution)/shard_map/all_gather | solution.py:174
  215.5 50.4 %conditional.2 = (f32[1,4,256]{2,1,0:T(4,128)S(1)}, f32[1,4,256,128]{3,2,1,0:T(8,128)S(1)}) conditional(s32[]{:T(128)} %convert_element_type.81, () %tuple.24, (s32[8192]{0:T(1024)S(1)}, s32[256]{0:T(256)S(1)}, s32[8192]{0:T(1024)S(1)}, s32[256]{0:T(256)S(1)}, bf16[512,512]{0,1:T(8,128)(2,1)S(1)}, /*index=5*/bf16[8192,128]{0,1:T(8,128)(2,1)}, ...), branch_computations={%region_9.10_spmd, %region_10.13_spmd} | conditional | flops 4393532416 | bytes 114649104 | solution.py:200
  215.5 5.6 %compare_and_fusion = pred[256,8192]{0,1:T(8,128)(4,1)S(1)} fusion(s32[256]{0:T(256)S(1)} %get-tuple-element.33, s32[256]{0:T(256)S(1)} %get-tuple-element.31, s32[8192]{0:T(1024)S(1)} %get-tuple-element.32, s32[8192]{0:T(1024)S(1)} %get-tuple-element.30), kind=kLoop, calls=%fused_computation.10 | loop fusion | flops 6291456 | bytes 2164736 | tf_op jit(solution)/shard_map/cond/branch_1_fun/and | solution.py:68
  221.1 15.1 %fusion = (f32[4,256]{1,0:T(4,128)S(1)}, f32[8192,256,4]{1,0,2:T(8,128)}) fusion(pred[256,8192]{0,1:T(8,128)(4,1)S(1)} %compare_and_fusion, bf16[256,4,128]{0,2,1:T(8,128)(2,1)S(1)} %bitcast.135, bf16[8192,128]{0,1:T(8,128)(2,1)} %get-tuple-element.86), kind=kOutput, calls=%fused_computation.2 | convolution fusion | flops 2172648448 | bytes 38014976 | tf_op jit(solution)/shard_map/cond/branch_1_fun/qkgd,nkd->kgqn/dot_general | solution.py:62
  236.2 15.2 %fusion.12 = f32[1,4,256,128]{3,2,1,0:T(8,128)S(1)} fusion(bf16[8192,128]{1,0:T(8,128)(2,1)} %get-tuple-element.36, f32[8192,256,4]{1,0,2:T(8,128)} %get-tuple-element.103, f32[4,256]{1,0:T(4,128)S(1)} %broadcast_maximum_fusion, pred[256,8192]{0,1:T(8,128)(4,1)S(1)} %compare_and_fusion), kind=kOutput, calls=%fused_computation.14 | convolution fusion | flops 2181038080 | bytes 38277120 | tf_op jit(solution)/shard_map/cond/branch_1_fun/kgqn,nkd->kgqd/dot_general | solution.py:76
  251.4 14.5 %fusion.4 = f32[4,256]{1,0:T(4,128)S(1)} fusion(f32[8192,256,4]{1,0,2:T(8,128)} %get-tuple-element.103, f32[4,256]{1,0:T(4,128)S(1)} %broadcast_maximum_fusion, pred[256,8192]{0,1:T(8,128)(4,1)S(1)} %compare_and_fusion), kind=kLoop, calls=%fused_computation.6 | loop fusion | flops 33553408 | bytes 35659776 | tf_op jit(solution)/shard_map/cond/branch_1_fun/reduce_sum | solution.py:74
  265.9 0.2 fusion.58
  266.1 0.2 copy.66
  266.4 50.8 %conditional.3 = (f32[1,4,256]{2,1,0:T(4,128)S(1)}, f32[1,4,256,128]{3,2,1,0:T(8,128)S(1)}) conditional(s32[]{:T(128)} %convert_element_type.94, () %tuple.26, (s32[8192]{0:T(1024)S(1)}, s32[256]{0:T(256)S(1)}, s32[8192]{0:T(1024)S(1)}, s32[256]{0:T(256)S(1)}, bf16[512,512]{0,1:T(8,128)(2,1)S(1)}, /*index=5*/bf16[8192,128]{0,1:T(8,128)(2,1)}, ...), branch_computations={%region_15.16_spmd, %region_16.19_spmd} | conditional | flops 4393532416 | bytes 114649104 | solution.py:200
  266.6 5.7 %compare_and_fusion.1 = pred[256,8192]{0,1:T(8,128)(4,1)S(1)} fusion(s32[256]{0:T(256)S(1)} %get-tuple-element.40, s32[256]{0:T(256)S(1)} %get-tuple-element.38, s32[8192]{0:T(1024)S(1)} %get-tuple-element.39, s32[8192]{0:T(1024)S(1)} %get-tuple-element.37), kind=kLoop, calls=%fused_computation.28 | loop fusion | flops 6291456 | bytes 2164736 | tf_op jit(solution)/shard_map/cond/branch_1_fun/and | solution.py:68
  272.3 15.1 %fusion.19 = (f32[4,256]{1,0:T(4,128)S(1)}, f32[8192,256,4]{1,0,2:T(8,128)}) fusion(pred[256,8192]{0,1:T(8,128)(4,1)S(1)} %compare_and_fusion.1, bf16[256,4,128]{0,2,1:T(8,128)(2,1)S(1)} %bitcast.136, bf16[8192,128]{0,1:T(8,128)(2,1)} %get-tuple-element.93), kind=kOutput, calls=%fused_computation.20 | convolution fusion | flops 2172648448 | bytes 38014976 | tf_op jit(solution)/shard_map/cond/branch_1_fun/qkgd,nkd->kgqn/dot_general | solution.py:62
  287.5 15.2 %fusion.31 = f32[1,4,256,128]{3,2,1,0:T(8,128)S(1)} fusion(bf16[8192,128]{1,0:T(8,128)(2,1)} %get-tuple-element.43, f32[8192,256,4]{1,0,2:T(8,128)} %get-tuple-element.105, f32[4,256]{1,0:T(4,128)S(1)} %broadcast_maximum_fusion.1, pred[256,8192]{0,1:T(8,128)(4,1)S(1)} %compare_and_fusion.1), kind=kOutput, calls=%fused_computation.32 | convolution fusion | flops 2181038080 | bytes 38277120 | tf_op jit(solution)/shard_map/cond/branch_1_fun/kgqn,nkd->kgqd/dot_general | solution.py:76
  302.6 14.5 %fusion.23 = f32[4,256]{1,0:T(4,128)S(1)} fusion(f32[8192,256,4]{1,0,2:T(8,128)} %get-tuple-element.105, f32[4,256]{1,0:T(4,128)S(1)} %broadcast_maximum_fusion.1, pred[256,8192]{0,1:T(8,128)(4,1)S(1)} %compare_and_fusion.1), kind=kLoop, calls=%fused_computation.24 | loop fusion | flops 33553408 | bytes 35659776 | tf_op jit(solution)/shard_map/cond/branch_1_fun/reduce_sum | solution.py:74
  317.1 0.2 fusion.59
  317.4 0.2 copy.68
  317.6 2.2 copy.84
  319.8 3.4 %copy.69 = bf16[64,128,128]{2,0,1:T(8,128)(2,1)} copy(bf16[64,128,128]{1,0,2:T(8,128)(2,1)S(1)} %bitcast.127) | data formatting | bytes 4194304 | tf_op jit(solution)/shard_map/reshape | solution.py:209
  323.2 2.0 fusion.51
  325.2 0.7 copy.71
  325.9 2.8 fusion.55
  328.7 0.7 copy.72
  329.4 0.1 copy_bitcast_fusion
  329.5 0.8 pad_maximum_fusion.1
  (24 shorter events, 0.2 us)
Async XLA Ops:
  7.2 46.4 %all-gather.6.cloned.1.call-start = ((), (), s32[]{:S(2)}) async-start(), calls=%async_computation | async-start | bytes 2949120 | tf_op jit(solution)/shard_map/all_gather | solution.py:109
  7.9 102.1 %all-gather.8.cloned.1.call-start = ((), (), s32[]{:S(2)}) async-start(), calls=%async_computation.1 | async-start | bytes 4177920 | tf_op jit(solution)/shard_map/all_gather | solution.py:121
  11.5 154.0 %all-gather.12.cloned.1.call-start = ((), (), s32[]{:S(2)}) async-start(), calls=%async_computation.3 | async-start | bytes 2228224 | tf_op jit(solution)/shard_map/all_gather | solution.py:173
  55.9 59.7 %copy-start.1 = (f32[128]{0:T(128)S(1)}, f32[128]{0:T(128)}, u32[]{:S(2)}) copy-start(f32[128]{0:T(128)} %param.19) | copy-start | bytes 1540
  55.9 66.7 %copy-start.3 = (s32[64]{0:T(128)S(1)}, s32[64]{0:T(128)}, u32[]{:S(2)}) copy-start(s32[64]{0:T(128)} %param.21) | copy-start | bytes 772
  115.4 7.9 %copy-start = (f32[512,768]{1,0:T(8,128)}, f32[512,768]{1,0:T(8,128)S(1)}, u32[]{:S(2)}) copy-start(f32[512,768]{1,0:T(8,128)S(1)} %fusion.41) | copy-start | bytes 4718596
  115.4 11.2 %copy-start.2 = (f32[128]{0:T(128)S(1)}, f32[128]{0:T(128)}, u32[]{:S(2)}) copy-start(f32[128]{0:T(128)} %param.18) | copy-start | bytes 1540
  117.0 98.5 %all-gather.10.cloned.1.call-start = ((), (), s32[]{:S(2)}) async-start(), calls=%async_computation.2 | async-start | bytes 2228224 | tf_op jit(solution)/shard_map/all_gather | solution.py:174
Sparse Core Ops, SparseCore 0:
  9.6 43.8 all-gather.5
  56.6 53.3 all-gather.7
  117.1 48.3 all-gather.11
  168.3 47.1 all-gather.9
where the time goes:
time: 341 us; the launch traced here: 337 us
  waiting for transfers between devices  179 us (52%)
  matrix products  70.8 us (21%)
  other arithmetic  55.6 us (16%)
  between operations  19 us (6%)
  local copies, waits for them, and re-layouts  12 us (4%)
    all_gather x1, waiting for transfers between devices, shards(): lax.all_gather(server_block, 'seq', axis=0, tiled=True)  54 us
    all_gather x1, waiting for transfers between devices, shards(): value_piece = lax.all_gather(values, 'seq', axis=0, tiled=True)  50 us
    all_gather x1, waiting for transfers between devices, shards(): gathered = lax.all_gather(hidden, 'tp', axis=1, tiled=True)  37.8 us
    all_gather x1, waiting for transfers between devices, shards(): key_piece = lax.all_gather(key_rows, 'seq', axis=0, tiled=True)  36.3 us
    dot_general x2, matrix products, attend(): jnp.einsum('kgqn,nkd->kgqd', probs, value_piece.reshape(key_count, kv_hea...  30.3 us
    dot_general x2, matrix products, attend(): jnp.einsum('qkgd,nkd->kgqn', query_block.reshape(half_rows, kv_heads, gro...  30.3 us
    reduce_sum x2, other arithmetic, attend(): denominator = jnp.sum(weights, axis=-1)  29 us
    and x2, other arithmetic, attend(): (key_segments[None, :] == query_segments[:, None]) & (key_slots[None, :]...  11.2 us
  transfers between devices with their start and end apart: 4, of which 4 were waited for; matrix products, arithmetic and copies ran while one was open for 5% of the time, Pallas kernels for 0%

commit v1 on v0

v1 whole, which is shorter than its diff:
```python
import math

import jax
import jax.numpy as jnp
import numpy as np
from jax import lax
from jax.experimental import pallas as pl
from jax.experimental.pallas import tpu as pltpu
from jax.sharding import PartitionSpec as P

T = 512
F = 320
D = 2560
WR = 160
HD = 128
G = 4
NC = 768
PAGE = 128
PAGES = 64
NSEG = 8
SEQ = 16
TP = 8
EPS = 1e-6
EXCLUDED = -1e30
HR = 640
MESH = pl.DeviceIdType.MESH
SCALE = HD**-0.5 * math.log2(math.e)
VE = HD + 16


def kernel(
    hid_ref,
    gain_ref,
    wq_ref,
    wk_ref,
    wv_ref,
    qg_ref,
    kg_ref,
    freq_ref,
    len_ref,
    pt_ref,
    out_ref,
    kc_ref,
    vc_ref,
    hall,
    wall,
    kv,
    hn,
    qt,
    acc,
    mx,
    cosr,
    sinr,
    startr,
    ssq,
    h_send,
    h_recv,
    w_send,
    w_recv,
    kv_send,
    kv_recv,
):
    s = lax.axis_index("seq")
    t = lax.axis_index("tp")
    yh, x, c = s // 8, (s // 2) % 4, s % 2
    yl, z = t // 4, t % 4

    def seq_rank(dx, dy, dc):
        return ((yh + dy) % 2) * 8 + ((x + dx) % 4) * 2 + (c + dc) % 2

    def tp_rank(dz, dy):
        return ((yl + dy) % 2) * 4 + (z + dz) % 4

    sib = {"seq": seq_rank(0, 0, 1), "tp": t}
    xp = {"seq": seq_rank(1, 0, 0), "tp": t}
    xm = {"seq": seq_rank(3, 0, 0), "tp": t}
    yhp = {"seq": seq_rank(0, 1, 0), "tp": t}
    zp = {"seq": s, "tp": tp_rank(1, 0)}
    zm = {"seq": s, "tp": tp_rank(3, 0)}
    ylp = {"seq": s, "tp": tp_rank(0, 1)}
    barrier = pltpu.get_barrier_semaphore()
    for peer in (sib, xp, xm, yhp, zp, zm, ylp):
        pl.semaphore_signal(barrier, inc=1, device_id=peer, device_id_type=MESH)

    hall[t, 0:T, :] = hid_ref[:, 0:256]
    for q in range(4):
        hall[t, T : T + 128, 64 * q : 64 * q + 64] = hid_ref[128 * q : 128 * q + 128, 256:320]
    own_w = pl.ds(pl.multiple_of(s * WR, 16), WR)
    wall[own_w, 0:512] = wq_ref[...].astype(jnp.bfloat16)
    wall[own_w, 512:640] = wk_ref[...].astype(jnp.bfloat16)
    wall[own_w, 640:768] = wv_ref[...].astype(jnp.bfloat16)

    pl.semaphore_wait(barrier, 7)

    started = []

    class Gather:
        def __init__(self, region, send, recv):
            self.region, self.send, self.recv, self.sends = region, send, recv, 0

        def go(self, rank, half, role, peer):
            ref = self.region(rank, half)
            copy = pltpu.make_async_remote_copy(
                src_ref=ref,
                dst_ref=ref,
                send_sem=self.send.at[self.sends],
                recv_sem=self.recv.at[role],
                device_id=peer,
                device_id_type=MESH,
            )
            self.sends += 1
            copy.start()
            started.append(copy)

        def wait(self, rank, half, role):
            ref = self.region(rank, half)
            pltpu.make_async_remote_copy(
                src_ref=ref,
                dst_ref=ref,
                send_sem=self.send.at[0],
                recv_sem=self.recv.at[role],
                device_id=sib,
                device_id_type=MESH,
            ).wait_recv()

    def h_region(rank, half):
        if half is None:
            return hall.at[rank]
        return hall.at[rank, pl.ds(half * (HR // 2), HR // 2), :]

    def w_region(rank, half):
        if half is None:
            return wall.at[pl.ds(pl.multiple_of(rank * WR, 16), WR), :]
        return wall.at[pl.ds(pl.multiple_of(rank * WR + half * (WR // 2), 16), WR // 2), :]

    def kv_region(rank, half):
        if half is None:
            return kv.at[pl.ds(rank * 8, 8)]
        return kv.at[pl.ds(rank * 8 + half * 4, 4)]

    seq_roles = [(0, 1, None), (3, 0, None), (3, 1, None), (1, 0, None), (1, 1, None), (2, 0, 0), (2, 1, 0), (2, 0, 1), (2, 1, 1)]
    seq_forward = {
        0: ((None, 2, xp), (None, 4, xm)),
        1: ((0, 5, xp),),
        2: ((0, 6, xp),),
        3: ((1, 7, xm),),
        4: ((1, 8, xm),),
    }

    def seq_begin(g):
        rank = seq_rank(0, 0, 0)
        g.go(rank, None, 0, yhp)
        g.go(rank, None, 1, xp)
        g.go(rank, None, 3, xm)
        g.go(rank, None, 10, sib)

    def seq_pass(g, role):
        dx, dy, half = seq_roles[role]
        rank = seq_rank(dx, dy, 0)
        g.wait(rank, half, role)
        for part, to, peer in seq_forward.get(role, ()):
            g.go(rank, part, to, peer)
        g.go(rank, half, 11 + role, sib)

    def seq_sib(g, role):
        if role is None:
            g.wait(seq_rank(0, 0, 1), None, 10)
        else:
            dx, dy, half = seq_roles[role]
            g.wait(seq_rank(dx, dy, 1), half, 11 + role)

    tp_roles = [(0, 1, None), (3, 0, None), (3, 1, None), (1, 0, None), (1, 1, None), (2, 0, 0), (2, 0, 1), (2, 1, 0), (2, 1, 1)]
    tp_forward = {
        0: ((None, 2, zp), (None, 4, zm)),
        1: ((0, 5, zp),),
        3: ((1, 6, zm),),
        5: ((0, 7, ylp),),
        6: ((1, 8, ylp),),
    }

    def tp_pass(g, role):
        dz, dy, half = tp_roles[role]
        rank = tp_rank(dz, dy)
        g.wait(rank, half, role)
        for part, to, peer in tp_forward.get(role, ()):
            g.go(rank, part, to, peer)

    gh = Gather(h_region, h_send, h_recv)
    gw = Gather(w_region, w_send, w_recv)
    gk = Gather(kv_region, kv_send, kv_recv)

    gh.go(t, None, 0, ylp)
    gh.go(t, None, 1, zp)
    gh.go(t, None, 3, zm)
    seq_begin(gw)

    def start_of(slots):
        start = jnp.zeros_like(slots)
        end = jnp.int32(0)
        for i in range(NSEG):
            end = end + len_ref[i]
            start = jnp.where(slots >= end, end, start)
        return start

    rows = s * T + lax.broadcasted_iota(jnp.int32, (T, HD), 0)
    position = (rows - start_of(rows)).astype(jnp.float32)
    angles = position * freq_ref[...]
    cosr[...] = jnp.cos(angles)
    lane = lax.broadcasted_iota(jnp.int32, (T, HD), 1)
    sine = jnp.sin(angles)
    sinr[...] = jnp.where(lane < HD // 2, -sine, sine)
    slots = s * T + lax.broadcasted_iota(jnp.int32, (8, T), 1)
    startr[...] = start_of(slots)

    per = T // PAGE
    source = [jnp.int32(0)] * per
    for b in range(PAGES):
        page = pt_ref[b] - s * per
        row = (b // per) * 2 * per + b % per
        source = [jnp.where(page == i, row, f) for i, f in enumerate(source)]

    ssq[...] = jnp.zeros_like(ssq)

    def add_squares(rank):
        v = hall[rank, 0:T, :].astype(jnp.float32)
        v = v * v
        ssq[...] += v[:, 0:HD] + v[:, HD:]

    add_squares(t)
    tp_pass(gh, 0)
    seq_pass(gw, 0)
    tp_pass(gh, 1)
    tp_pass(gh, 3)
    seq_pass(gw, 1)
    seq_pass(gw, 3)
    seq_sib(gw, None)
    tp_pass(gh, 5)
    tp_pass(gh, 6)
    seq_pass(gw, 2)
    seq_pass(gw, 4)
    for dz, dy in ((0, 1), (1, 0), (3, 0), (2, 0)):
        add_squares(tp_rank(dz, dy))
    for role in (5, 7, 6, 8):
        seq_pass(gw, role)
    for role in range(9):
        seq_sib(gw, role)
    tp_pass(gh, 2)
    add_squares(tp_rank(3, 1))
    tp_pass(gh, 4)
    add_squares(tp_rank(1, 1))
    tp_pass(gh, 7)
    tp_pass(gh, 8)
    add_squares(tp_rank(2, 1))

    half_lane = lax.broadcasted_iota(jnp.int32, (128, 128), 1) < 64
    for pair in range(TP // 2):
        for col in range(2):
            lanes = slice(128 * col, 128 * col + 128)
            a = hall[2 * pair, T : T + 128, lanes].astype(jnp.float32)
            b = hall[2 * pair + 1, T : T + 128, lanes].astype(jnp.float32)
            low = jnp.where(half_lane, a, pltpu.roll(b, 64, 1))
            high = jnp.where(half_lane, pltpu.roll(a, 64, 1), b)
            for q, v in ((2 * col, low), (2 * col + 1, high)):
                where = slice(128 * q, 128 * q + 128)
                ssq[where, :] += v * v
                hn[where, 2048 + 128 * pair : 2176 + 128 * pair] = v.astype(jnp.bfloat16)

    scale = lax.rsqrt(jnp.sum(ssq[...], axis=1, keepdims=True) * (1.0 / D) + EPS)
    for i in range(TP):
        v = hall[i, 0:T, :].astype(jnp.float32) * scale
        hn[:, 256 * i : 256 * i + 256] = (v * gain_ref[:, 256 * i : 256 * i + 256]).astype(jnp.bfloat16)
    v = hn[:, 2048:].astype(jnp.float32) * scale
    hn[:, 2048:] = (v * gain_ref[:, 2048:]).astype(jnp.bfloat16)

    def project(lo, hi):
        total = None
        for i in range(TP):
            w = wall[F * i : F * i + 256, lo:hi]
            part = jnp.dot(hn[:, 256 * i : 256 * i + 256], w, preferred_element_type=jnp.float32)
            total = part if total is None else total + part
        for i in range(2):
            w = jnp.concatenate([wall[F * j + 256 : F * j + 320, lo:hi] for j in range(4 * i, 4 * i + 4)], axis=0)
            at = 2048 + 256 * i
            total = total + jnp.dot(hn[:, at : at + 256], w, preferred_element_type=jnp.float32)
        return total

    def norm_rotate(u, gain):
        mean = jnp.sum(u * u, axis=1, keepdims=True) * (1.0 / HD)
        u = u * lax.rsqrt(mean + EPS) * gain
        return u * cosr[...] + pltpu.roll(u, HD // 2, 1) * sinr[...]

    kvp = project(512, 768)
    keys = norm_rotate(kvp[:, 0:HD], kg_ref[...]).astype(jnp.bfloat16)
    vt = kvp[:, HD:].T.astype(jnp.bfloat16)
    for i in range(T // PAGE):
        kv[s * 8 + i] = keys[PAGE * i : PAGE * i + PAGE, :]
        kv[s * 8 + per + i] = vt[:, PAGE * i : PAGE * i + PAGE]
    seq_begin(gk)

    for pair in range(G // 2):
        qp = project(256 * pair, 256 * pair + 256)
        for i in range(2):
            u = norm_rotate(qp[:, HD * i : HD * i + HD], qg_ref[...]).astype(jnp.bfloat16)
            qt[2 * pair + i] = u.astype(jnp.float32).T.astype(jnp.bfloat16)

    ones = jnp.where(lax.broadcasted_iota(jnp.int32, (VE - HD, T), 0) == 0, 1.0, 0.0).astype(jnp.bfloat16)

    def attend(rank, diagonal):
        keys = jnp.concatenate([kv[rank * 8 + i] for i in range(per)], axis=0)
        vals = jnp.concatenate([kv[rank * 8 + per + i] for i in range(per)], axis=1)
        vals = jnp.concatenate([vals, ones], axis=0)

        def head(h, carry):
            scores = jnp.dot(keys, qt[h], preferred_element_type=jnp.float32)
            key_slot = rank * T + lax.broadcasted_iota(jnp.int32, (T, T), 0)
            allowed = key_slot >= startr[0:1, :]
            if diagonal:
                query_slot = rank * T + lax.broadcasted_iota(jnp.int32, (T, T), 1)
                allowed = allowed & (key_slot <= query_slot)
            scores = jnp.where(allowed, scores, EXCLUDED)
            top = jnp.max(scores, axis=0, keepdims=True)
            if not diagonal:
                old = mx[h]
                top = jnp.maximum(old, top)
            probs = jnp.exp2((scores - top) * SCALE).astype(jnp.bfloat16)
            sums = jnp.dot(vals, probs, preferred_element_type=jnp.float32)
            if diagonal:
                acc[h] = sums
            else:
                acc[h] = acc[h] * jnp.exp2((old - top) * SCALE) + sums
            mx[h] = top
            return carry

        lax.fori_loop(0, G, head, 0)

    def attend_all(offsets):
        def one(k, carry):
            rank = seq_rank(*offsets[0])
            for i in range(1, len(offsets)):
                rank = jnp.where(k == i, seq_rank(*offsets[i]), rank)

            @pl.when((rank < s) & (rank + 8 >= s))
            def _():
                attend(rank, False)

            return carry

        lax.fori_loop(0, len(offsets), one, 0)

    attend(s, True)
    seq_pass(gk, 0)
    seq_pass(gk, 1)
    seq_pass(gk, 3)
    seq_sib(gk, None)
    attend_all([(0, 0, 1), (3, 0, 0), (1, 0, 0), (0, 1, 0)])
    seq_pass(gk, 2)
    seq_pass(gk, 4)
    for role in (0, 1, 3):
        seq_sib(gk, role)
    attend_all([(3, 0, 1), (1, 0, 1), (0, 1, 1), (3, 1, 0), (1, 1, 0)])
    for role in (5, 7, 6, 8):
        seq_pass(gk, role)
    for role in (2, 4):
        seq_sib(gk, role)
    attend_all([(3, 1, 1), (1, 1, 1), (2, 0, 0), (2, 1, 0)])
    for role in (5, 6, 7, 8):
        seq_sib(gk, role)
    attend_all([(2, 0, 1), (2, 1, 1)])

    for h in range(G):
        o = acc[h, 0:HD, :] / acc[h, HD : HD + 1, :]
        out_ref[:, HD * h : HD * h + HD] = o.T.astype(jnp.bfloat16)

    for i in range(per):
        kc_ref[i, 0] = kv[source[i]]
        page = kv[source[i] + per]
        vc_ref[i, 0] = page.astype(jnp.float32).T.astype(jnp.bfloat16)

    for copy in started:
        copy.wait_send()


def shards(hidden, norm_gain, query_weight, key_weight, value_weight, query_gain, key_gain, lengths, page_table):
    by_shard = norm_gain.reshape(TP, F)
    gain = jnp.concatenate([by_shard[:, :256].reshape(1, -1), by_shard[:, 256:].reshape(1, -1)], axis=1)
    half = 1000000.0 ** -(np.arange(HD // 2, dtype=np.float32) * np.float32(2.0 / HD))
    freq = jnp.asarray(np.concatenate([half, half])[None, :].astype(np.float32))
    vmem = pl.BlockSpec(memory_space=pltpu.VMEM)
    smem = pl.BlockSpec(memory_space=pltpu.SMEM)
    return pl.pallas_call(
        kernel,
        out_shape=(
            jax.ShapeDtypeStruct((T, G * HD), jnp.bfloat16),
            jax.ShapeDtypeStruct((T // PAGE, 1, PAGE, HD), jnp.bfloat16),
            jax.ShapeDtypeStruct((T // PAGE, 1, PAGE, HD), jnp.bfloat16),
        ),
        in_specs=[vmem] * 8 + [smem] * 2,
        out_specs=(vmem,) * 3,
        scratch_shapes=[
            pltpu.VMEM((TP, HR, 256), jnp.bfloat16),
            pltpu.VMEM((D, NC), jnp.bfloat16),
            pltpu.VMEM((SEQ * 8, PAGE, HD), jnp.bfloat16),
            pltpu.VMEM((T, D), jnp.bfloat16),
            pltpu.VMEM((G, HD, T), jnp.bfloat16),
            pltpu.VMEM((G, VE, T), jnp.float32),
            pltpu.VMEM((G, 1, T), jnp.float32),
            pltpu.VMEM((T, HD), jnp.float32),
            pltpu.VMEM((T, HD), jnp.float32),
            pltpu.VMEM((8, T), jnp.int32),
            pltpu.VMEM((T, HD), jnp.float32),
            pltpu.SemaphoreType.DMA((9,)),
            pltpu.SemaphoreType.DMA((9,)),
            pltpu.SemaphoreType.DMA((20,)),
            pltpu.SemaphoreType.DMA((20,)),
            pltpu.SemaphoreType.DMA((20,)),
            pltpu.SemaphoreType.DMA((20,)),
        ],
        compiler_params=pltpu.CompilerParams(
            collective_id=0, has_side_effects=True, vmem_limit_bytes=48 * 1024 * 1024
        ),
        cost_estimate=pl.CostEstimate(flops=7 * 10**9, bytes_accessed=4 * 10**6, transcendentals=10**7),
    )(
        hidden,
        gain,
        query_weight,
        key_weight,
        value_weight,
        query_gain.reshape(1, HD),
        key_gain.reshape(1, HD),
        freq,
        lengths,
        page_table,
    )


def solution(mesh):
    return jax.shard_map(
        shards,
        mesh=mesh,
        in_specs=(
            P("seq", "tp"),
            P(),
            P("seq", "tp"),
            P("seq", "tp"),
            P("seq", "tp"),
            P(),
            P(),
            P(),
            P(),
        ),
        out_specs=(P("seq", "tp"), P("seq", "tp", None, None), P("seq", "tp", None, None)),
        check_vma=False,
    )
```

time: 341 us -> 78.6 us (0.23); the launches traced: 337 us -> 78.5 us
  waiting for transfers between devices: 179 us -> 0 us
  Pallas kernels: 0 us -> 73.4 us
  matrix products: 70.8 us -> 0 us
  other arithmetic: 55.6 us -> 0.01 us
  between operations: 19 us -> 0.79 us
  local copies, waits for them, and re-layouts: 12 us -> 4.29 us
    all_gather x4 -> x0, waiting for transfers between devices: 178 us -> none  [the longest x1 54 us: shards(): lax.all_gather(server_block, 'seq', axis=0, tiled=True)]
    pallas_call x0 -> x1, Pallas kernels: none -> 73.4 us  [shards(): pl.pallas_call(kernel, out_shape=(jax.ShapeDtypeStruct((T, G * HD), jnp.b...]
    dot_general x7 -> x0, matrix products: 70.8 us -> none  [the longest x2 30.3 us: attend(): jnp.einsum('kgqn,nkd->kgqd', probs, value_piece.reshape(key_count, kv_hea...]
    reduce_sum x11 -> x0, other arithmetic: 34 us -> none  [the longest x2 29 us: attend(): denominator = jnp.sum(weights, axis=-1)]
    and x2 -> x0, other arithmetic: 11.2 us -> none  [attend(): (key_segments[None, :] == query_segments[:, None]) & (key_slots[None, :]...]
    another operation x8 -> x0, other arithmetic: 5.03 us -> none
    slice x9 -> x1, local copies, waits for them, and re-layouts: 3.76 us -> 0.01 us  [shards(): by_shard[:, 256:].reshape(1, -1)]
  transfers between devices with their start and end apart: 4 -> 0, of which waited for: 4 -> 0; matrix products, arithmetic and copies ran while one was open for 5% -> 0% of each run, Pallas kernels for 0% -> 0%
where the time goes in v1:
time: 78.6 us; the launch traced here: 78.5 us
  Pallas kernels  73.4 us (93%)
  local copies, waits for them, and re-layouts  4.29 us (5%)
  between operations  0.79 us (1%)
    pallas_call x1, Pallas kernels, shards(): pl.pallas_call(kernel, out_shape=(jax.ShapeDtypeStruct((T, G * HD), jnp.b...  73.4 us
    unnamed x22, local copies, waits for them, and re-layouts  3.43 us

profile of v1, /device:TPU:24, one launch (start us, length us, event | category | flops | bytes accessed | tf_op | source)
XLA Modules:
  0.0 78.5 jit_solution(957496033885770941)
XLA Ops:
  0.6 0.8 reshape.21
  1.4 0.1 reshape.23
  1.5 0.0 copy-start
  1.5 0.0 copy-start.1
  1.6 0.0 copy-start.2
  1.6 0.0 copy-start.3
  1.6 0.0 copy-start.4
  1.6 0.0 copy-start.5
  1.6 0.0 copy-start.6
  1.6 0.0 copy-start.7
  1.6 1.3 %copy.13.hid_ref = bf16[512,320]{1,0:T(8,128)(2,1)S(1)} copy(bf16[512,320]{0,1:T(8,128)(2,1)} %param.10) | data formatting | bytes 655360 | tf_op args[0]
  2.9 0.0 copy-done
  2.9 0.0 copy-done.1
  2.9 0.0 copy-done.2
  2.9 0.0 copy-done.3
  2.9 0.0 copy-done.4
  2.9 0.0 copy-done.5
  3.0 0.0 copy-done.6
  3.0 0.0 copy-done.7
  3.0 73.4 %shard_map.121 = (bf16[512,512]{1,0:T(8,128)(2,1)S(1)}, bf16[4,1,128,128]{3,2,1,0:T(8,128)(2,1)S(1)}, bf16[4,1,128,128]{3,2,1,0:T(8,128)(2,1)S(1)}) custom-call(bf16[512,320]{1,0:T(8,128)(2,1)S(1)} %copy.13.hid_ref, f32[1,2560]{1,0:T(1,128)S(1)} %pad_maximum_fusion.gain_ref, f32[160,512]{1,0:T(8,128)S(1)} %copy-done, f32[160,128]{1,0:T(8,128)S(1)} %copy-done.1, ...), custom_call_target="tpu_custom_call" | custom-call | flops 7000000000 | bytes 4000000 | tf_op jit(solution)/shard_map/pallas_call | solution.py:390
  76.3 0.8 %copy.18 = bf16[512,512]{1,0:T(8,128)(2,1)} copy(bf16[512,512]{1,0:T(8,128)(2,1)S(1)} %get-tuple-element.6) | data formatting | bytes 1048576
  77.1 0.7 copy.19
  77.8 0.7 copy.20
  (4 shorter events, 0.0 us)
Async XLA Ops:
  1.5 1.4 %copy-start = (f32[160,512]{1,0:T(8,128)S(1)}, f32[160,512]{1,0:T(8,128)}, u32[]{:S(2)}) copy-start(f32[160,512]{1,0:T(8,128)} %wq_ref.1) | copy-start | bytes 983044
  1.5 1.4 %copy-start.1 = (f32[160,128]{1,0:T(8,128)S(1)}, f32[160,128]{1,0:T(8,128)}, u32[]{:S(2)}) copy-start(f32[160,128]{1,0:T(8,128)} %wk_ref.1) | copy-start | bytes 245764
  1.6 1.4 %copy-start.2 = (f32[160,128]{1,0:T(8,128)S(1)}, f32[160,128]{1,0:T(8,128)}, u32[]{:S(2)}) copy-start(f32[160,128]{1,0:T(8,128)} %wv_ref.1) | copy-start | bytes 245764
  1.6 1.4 %copy-start.3 = (f32[128]{0:T(128)S(1)}, f32[128]{0:T(128)}, u32[]{:S(2)}) copy-start(f32[128]{0:T(128)} %param.15) | copy-start | bytes 1540
  1.6 1.4 %copy-start.4 = (f32[128]{0:T(128)S(1)}, f32[128]{0:T(128)}, u32[]{:S(2)}) copy-start(f32[128]{0:T(128)} %param.16) | copy-start | bytes 1540
  1.6 1.4 %copy-start.5 = (s32[8]{0:T(128)S(1)}, s32[8]{0:T(128)}, u32[]{:S(2)}) copy-start(s32[8]{0:T(128)} %len_ref.1) | copy-start | bytes 100
  1.6 1.4 %copy-start.6 = (s32[64]{0:T(128)S(1)}, s32[64]{0:T(128)}, u32[]{:S(2)}) copy-start(s32[64]{0:T(128)} %pt_ref.1) | copy-start | bytes 772
  1.6 1.4 %copy-start.7 = (f32[1,128]{1,0:T(1,128)S(1)}, f32[1,128]{1,0:T(1,128)}, u32[]{:S(2)}) copy-start(f32[1,128]{1,0:T(1,128)} %constant.2.clone.freq_ref) | copy-start | bytes 1540

commit v2 on v1

--- a/solution.py
+++ b/solution.py
@@ -52,6 +52,8 @@
     cosr,
     sinr,
     startr,
+    other,
+    bounds,
     ssq,
     h_send,
     h_recv,
@@ -211,6 +213,21 @@
     sinr[...] = jnp.where(lane < HD // 2, -sine, sine)
     slots = s * T + lax.broadcasted_iota(jnp.int32, (8, T), 1)
     startr[...] = start_of(slots)
+    label = lax.broadcasted_iota(jnp.int32, (HD, T), 0)
+    lane_label = lax.broadcasted_iota(jnp.int32, (8, HD), 1)
+    query_slot = s * T + lax.broadcasted_iota(jnp.int32, (HD, T), 1)
+    mine = label >= NSEG
+    low = jnp.zeros((8, HD), jnp.int32)
+    high = jnp.zeros((8, HD), jnp.int32)
+    end = jnp.int32(0)
+    for i in range(NSEG):
+        begin, end = end, end + len_ref[i]
+        mine = mine | ((label == i) & (query_slot >= begin) & (query_slot < end))
+        low = jnp.where(lane_label == i, begin, low)
+        high = jnp.where(lane_label == i, end, high)
+    other[...] = jnp.where(mine, 0.0, EXCLUDED).astype(jnp.bfloat16)
+    bounds[0:1, :] = low[0:1, :]
+    bounds[1:2, :] = high[0:1, :]
 
     per = T // PAGE
     source = [jnp.int32(0)] * per
@@ -309,15 +326,27 @@
         keys = jnp.concatenate([kv[rank * 8 + i] for i in range(per)], axis=0)
         vals = jnp.concatenate([kv[rank * 8 + per + i] for i in range(per)], axis=1)
         vals = jnp.concatenate([vals, ones], axis=0)
-
-        def head(h, carry):
-            scores = jnp.dot(keys, qt[h], preferred_element_type=jnp.float32)
-            key_slot = rank * T + lax.broadcasted_iota(jnp.int32, (T, T), 0)
-            allowed = key_slot >= startr[0:1, :]
+        if not diagonal:
+            key_slot = rank * T + lax.broadcasted_iota(jnp.int32, (T, HD), 0)
+            member = (key_slot >= bounds[0:1, :]) & (key_slot < bounds[1:2, :])
+            keys = jnp.concatenate([keys, jnp.where(member, 1.0, 0.0).astype(jnp.bfloat16)], axis=1)
+
+        def score(h):
             if diagonal:
+                return jnp.dot(keys, qt[h], preferred_element_type=jnp.float32)
+            queries = jnp.concatenate([qt[h], other[...]], axis=0)
+            return jnp.dot(keys, queries, preferred_element_type=jnp.float32)
+
+        ahead = score(0)
+        for h in range(G):
+            scores = ahead
+            if h + 1 < G:
+                ahead = score(h + 1)
+            if diagonal:
+                key_slot = rank * T + lax.broadcasted_iota(jnp.int32, (T, T), 0)
                 query_slot = rank * T + lax.broadcasted_iota(jnp.int32, (T, T), 1)
-                allowed = allowed & (key_slot <= query_slot)
-            scores = jnp.where(allowed, scores, EXCLUDED)
+                allowed = (key_slot >= startr[0:1, :]) & (key_slot <= query_slot)
+                scores = jnp.where(allowed, scores, EXCLUDED)
             top = jnp.max(scores, axis=0, keepdims=True)
             if not diagonal:
                 old = mx[h]
@@ -329,9 +358,6 @@
             else:
                 acc[h] = acc[h] * jnp.exp2((old - top) * SCALE) + sums
             mx[h] = top
-            return carry
-
-        lax.fori_loop(0, G, head, 0)
 
     def attend_all(offsets):
         def one(k, carry):
@@ -407,6 +433,8 @@
             pltpu.VMEM((T, HD), jnp.float32),
             pltpu.VMEM((T, HD), jnp.float32),
             pltpu.VMEM((8, T), jnp.int32),
+            pltpu.VMEM((HD, T), jnp.bfloat16),
+            pltpu.VMEM((8, HD), jnp.int32),
             pltpu.VMEM((T, HD), jnp.float32),
             pltpu.SemaphoreType.DMA((9,)),
             pltpu.SemaphoreType.DMA((9,)),

time: 78.6 us -> 72.6 us (0.924)
  Pallas kernels: 73.4 us -> 67.3 us
    pallas_call x1, Pallas kernels: 73.4 us -> 67.3 us  [shards(): pl.pallas_call(kernel, out_shape=(jax.ShapeDtypeStruct((T, G * HD), jnp.b...]
where the time goes in v2:
time: 72.6 us; the launch traced here: 72.4 us
  Pallas kernels  67.3 us (93%)
  local copies, waits for them, and re-layouts  4.29 us (6%)
  between operations  0.79 us (1%)
    pallas_call x1, Pallas kernels, shards(): pl.pallas_call(kernel, out_shape=(jax.ShapeDtypeStruct((T, G * HD), jnp.b...  67.3 us
    unnamed x22, local copies, waits for them, and re-layouts  3.43 us

profile of v2, /device:TPU:24, one launch (start us, length us, event | category | flops | bytes accessed | tf_op | source)
XLA Modules:
  0.0 72.4 jit_solution(3265274497804609951)
XLA Ops:
  0.6 0.8 %reshape.21 = f32[8,320]{1,0:T(8,128)S(1)} reshape(f32[2560]{0:T(1024)} %param.11) | data formatting | bytes 20480 | tf_op jit(solution)/shard_map/reshape | solution.py:410
  1.4 0.1 reshape.23
  1.5 0.0 copy-start
  1.5 0.0 copy-start.1
  1.6 0.0 copy-start.2
  1.6 0.0 copy-start.3
  1.6 0.0 copy-start.4
  1.6 0.0 copy-start.5
  1.6 0.0 copy-start.6
  1.6 0.0 copy-start.7
  1.6 1.3 %copy.13.hid_ref = bf16[512,320]{1,0:T(8,128)(2,1)S(1)} copy(bf16[512,320]{0,1:T(8,128)(2,1)} %param.10) | data formatting | bytes 655360 | tf_op args[0]
  2.9 0.0 copy-done
  2.9 0.0 copy-done.1
  2.9 0.0 copy-done.2
  2.9 0.0 copy-done.3
  2.9 0.0 copy-done.4
  2.9 0.0 copy-done.5
  3.0 0.0 copy-done.6
  3.0 0.0 copy-done.7
  3.0 67.3 %shard_map.121 = (bf16[512,512]{1,0:T(8,128)(2,1)S(1)}, bf16[4,1,128,128]{3,2,1,0:T(8,128)(2,1)S(1)}, bf16[4,1,128,128]{3,2,1,0:T(8,128)(2,1)S(1)}) custom-call(bf16[512,320]{1,0:T(8,128)(2,1)S(1)} %copy.13.hid_ref, f32[1,2560]{1,0:T(1,128)S(1)} %pad_maximum_fusion.gain_ref, f32[160,512]{1,0:T(8,128)S(1)} %copy-done, f32[160,128]{1,0:T(8,128)S(1)} %copy-done.1, ...), custom_call_target="tpu_custom_call" | custom-call | flops 7000000000 | bytes 4000000 | tf_op jit(solution)/shard_map/pallas_call | solution.py:416
  70.3 0.8 %copy.18 = bf16[512,512]{1,0:T(8,128)(2,1)} copy(bf16[512,512]{1,0:T(8,128)(2,1)S(1)} %get-tuple-element.6) | data formatting | bytes 1048576
  71.1 0.7 copy.19
  71.8 0.7 copy.20
  (4 shorter events, 0.0 us)
Async XLA Ops:
  1.5 1.4 %copy-start = (f32[160,512]{1,0:T(8,128)S(1)}, f32[160,512]{1,0:T(8,128)}, u32[]{:S(2)}) copy-start(f32[160,512]{1,0:T(8,128)} %wq_ref.1) | copy-start | bytes 983044
  1.5 1.4 %copy-start.1 = (f32[160,128]{1,0:T(8,128)S(1)}, f32[160,128]{1,0:T(8,128)}, u32[]{:S(2)}) copy-start(f32[160,128]{1,0:T(8,128)} %wk_ref.1) | copy-start | bytes 245764
  1.6 1.4 %copy-start.2 = (f32[160,128]{1,0:T(8,128)S(1)}, f32[160,128]{1,0:T(8,128)}, u32[]{:S(2)}) copy-start(f32[160,128]{1,0:T(8,128)} %wv_ref.1) | copy-start | bytes 245764
  1.6 1.4 %copy-start.3 = (f32[128]{0:T(128)S(1)}, f32[128]{0:T(128)}, u32[]{:S(2)}) copy-start(f32[128]{0:T(128)} %param.15) | copy-start | bytes 1540
  1.6 1.4 %copy-start.4 = (f32[128]{0:T(128)S(1)}, f32[128]{0:T(128)}, u32[]{:S(2)}) copy-start(f32[128]{0:T(128)} %param.16) | copy-start | bytes 1540
  1.6 1.4 %copy-start.5 = (s32[8]{0:T(128)S(1)}, s32[8]{0:T(128)}, u32[]{:S(2)}) copy-start(s32[8]{0:T(128)} %len_ref.1) | copy-start | bytes 100
  1.6 1.4 %copy-start.6 = (s32[64]{0:T(128)S(1)}, s32[64]{0:T(128)}, u32[]{:S(2)}) copy-start(s32[64]{0:T(128)} %pt_ref.1) | copy-start | bytes 772
  1.6 1.4 %copy-start.7 = (f32[1,128]{1,0:T(1,128)S(1)}, f32[1,128]{1,0:T(1,128)}, u32[]{:S(2)}) copy-start(f32[1,128]{1,0:T(1,128)} %constant.2.clone.freq_ref) | copy-start | bytes 1540

commit v3 on v2

--- a/solution.py
+++ b/solution.py
@@ -30,7 +30,7 @@
 
 def kernel(
     hid_ref,
-    gain_ref,
+    gain_1d,
     wq_ref,
     wk_ref,
     wv_ref,
@@ -171,30 +171,40 @@
             dx, dy, half = seq_roles[role]
             g.wait(seq_rank(dx, dy, 1), half, 11 + role)
 
-    tp_roles = [(0, 1, None), (3, 0, None), (3, 1, None), (1, 0, None), (1, 1, None), (2, 0, 0), (2, 0, 1), (2, 1, 0), (2, 1, 1)]
+    tp_roles = {"zm": (3, 0), "zp": (1, 0), "y": (0, 1), "z2": (2, 0), "zmy": (3, 1), "zpy": (1, 1), "z2y": (2, 1)}
+    tp_index = {name: 2 * i for i, name in enumerate(tp_roles)}
     tp_forward = {
-        0: ((None, 2, zp), (None, 4, zm)),
-        1: ((0, 5, zp),),
-        3: ((1, 6, zm),),
-        5: ((0, 7, ylp),),
-        6: ((1, 8, ylp),),
+        ("zm", 0): (("z2", zp),),
+        ("zp", 1): (("z2", zm),),
+        ("y", 0): (("zmy", zp), ("zpy", zm)),
+        ("y", 1): (("zmy", zp), ("zpy", zm)),
+        ("z2", 0): (("z2y", ylp),),
+        ("z2", 1): (("z2y", ylp),),
     }
 
-    def tp_pass(g, role):
-        dz, dy, half = tp_roles[role]
-        rank = tp_rank(dz, dy)
-        g.wait(rank, half, role)
-        for part, to, peer in tp_forward.get(role, ()):
-            g.go(rank, part, to, peer)
+    def tp_pass(name, piece):
+        rank = tp_rank(*tp_roles[name])
+        gh.wait(rank, piece, tp_index[name] + piece)
+        for to, peer in tp_forward.get((name, piece), ()):
+            gh.go(rank, piece, tp_index[to] + piece, peer)
+
+    def tp_begin(name, piece, peer):
+        gh.go(t, piece, tp_index[name] + piece, peer)
 
     gh = Gather(h_region, h_send, h_recv)
     gw = Gather(w_region, w_send, w_recv)
     gk = Gather(kv_region, kv_send, kv_recv)
 
-    gh.go(t, None, 0, ylp)
-    gh.go(t, None, 1, zp)
-    gh.go(t, None, 3, zm)
-    seq_begin(gw)
+    tp_begin("zm", 0, zp)
+    tp_begin("zp", 1, zm)
+    tp_begin("y", 0, ylp)
+    gw.go(s, None, 0, yhp)
+    tp_begin("y", 1, ylp)
+    gw.go(s, None, 1, xp)
+    gw.go(s, None, 3, xm)
+    tp_begin("zm", 1, zp)
+    tp_begin("zp", 0, zm)
+    gw.go(s, None, 10, sib)
 
     def start_of(slots):
         start = jnp.zeros_like(slots)
@@ -244,30 +254,38 @@
         ssq[...] += v[:, 0:HD] + v[:, HD:]
 
     add_squares(t)
-    tp_pass(gh, 0)
-    seq_pass(gw, 0)
-    tp_pass(gh, 1)
-    tp_pass(gh, 3)
+    for name, piece in (("zm", 0), ("zp", 1)):
+        tp_pass(name, piece)
     seq_pass(gw, 1)
     seq_pass(gw, 3)
-    seq_sib(gw, None)
-    tp_pass(gh, 5)
-    tp_pass(gh, 6)
+    for name, piece in (("zm", 1), ("zp", 0), ("y", 0)):
+        tp_pass(name, piece)
+    seq_pass(gw, 0)
+    tp_pass("y", 1)
+    tp_pass("z2", 0)
+    seq_pass(gw, 5)
+    tp_pass("z2", 1)
+    seq_pass(gw, 7)
+    for dz, dy in ((0, 1), (1, 0), (3, 0), (2, 0)):
+        add_squares(tp_rank(dz, dy))
     seq_pass(gw, 2)
     seq_pass(gw, 4)
-    for dz, dy in ((0, 1), (1, 0), (3, 0), (2, 0)):
-        add_squares(tp_rank(dz, dy))
-    for role in (5, 7, 6, 8):
-        seq_pass(gw, role)
+    for name, piece in (("zmy", 0), ("zpy", 0), ("zmy", 1), ("zpy", 1)):
+        tp_pass(name, piece)
+    seq_pass(gw, 6)
+    seq_pass(gw, 8)
+    add_squares(tp_rank(3, 1))
+    add_squares(tp_rank(1, 1))
+    tp_pass("z2y", 0)
+    tp_pass("z2y", 1)
+    add_squares(tp_rank(2, 1))
+    seq_sib(gw, None)
     for role in range(9):
         seq_sib(gw, role)
-    tp_pass(gh, 2)
-    add_squares(tp_rank(3, 1))
-    tp_pass(gh, 4)
-    add_squares(tp_rank(1, 1))
-    tp_pass(gh, 7)
-    tp_pass(gh, 8)
-    add_squares(tp_rank(2, 1))
+
+    gain_row = gain_1d[...].reshape(1, D)
+    gain_ref = [gain_row[:, F * i : F * i + 256] for i in range(TP)]
+    gain_last = jnp.concatenate([gain_row[:, F * i + 256 : F * i + F] for i in range(TP)], axis=1)
 
     half_lane = lax.broadcasted_iota(jnp.int32, (128, 128), 1) < 64
     for pair in range(TP // 2):
@@ -285,9 +303,9 @@
     scale = lax.rsqrt(jnp.sum(ssq[...], axis=1, keepdims=True) * (1.0 / D) + EPS)
     for i in range(TP):
         v = hall[i, 0:T, :].astype(jnp.float32) * scale
-        hn[:, 256 * i : 256 * i + 256] = (v * gain_ref[:, 256 * i : 256 * i + 256]).astype(jnp.bfloat16)
+        hn[:, 256 * i : 256 * i + 256] = (v * gain_ref[i]).astype(jnp.bfloat16)
     v = hn[:, 2048:].astype(jnp.float32) * scale
-    hn[:, 2048:] = (v * gain_ref[:, 2048:]).astype(jnp.bfloat16)
+    hn[:, 2048:] = (v * gain_last).astype(jnp.bfloat16)
 
     def project(lo, hi):
         total = None
@@ -378,20 +396,23 @@
     seq_pass(gk, 1)
     seq_pass(gk, 3)
     seq_sib(gk, None)
-    attend_all([(0, 0, 1), (3, 0, 0), (1, 0, 0), (0, 1, 0)])
+    attend_all([(0, 0, 1), (0, 1, 0)])
     seq_pass(gk, 2)
     seq_pass(gk, 4)
     for role in (0, 1, 3):
         seq_sib(gk, role)
-    attend_all([(3, 0, 1), (1, 0, 1), (0, 1, 1), (3, 1, 0), (1, 1, 0)])
-    for role in (5, 7, 6, 8):
+    attend_all([(3, 0, 0), (1, 0, 0), (0, 1, 1)])
+    for role in (5, 7):
         seq_pass(gk, role)
-    for role in (2, 4):
+    attend_all([(3, 0, 1), (1, 0, 1), (3, 1, 0), (1, 1, 0), (2, 0, 0)])
+    for role in (6, 8):
+        seq_pass(gk, role)
+    for role in (2, 4, 5, 7):
         seq_sib(gk, role)
-    attend_all([(3, 1, 1), (1, 1, 1), (2, 0, 0), (2, 1, 0)])
-    for role in (5, 6, 7, 8):
+    attend_all([(3, 1, 1), (1, 1, 1), (2, 0, 1), (2, 1, 0)])
+    for role in (6, 8):
         seq_sib(gk, role)
-    attend_all([(2, 0, 1), (2, 1, 1)])
+    attend_all([(2, 1, 1)])
 
     for h in range(G):
         o = acc[h, 0:HD, :] / acc[h, HD : HD + 1, :]
@@ -407,8 +428,6 @@
 
 
 def shards(hidden, norm_gain, query_weight, key_weight, value_weight, query_gain, key_gain, lengths, page_table):
-    by_shard = norm_gain.reshape(TP, F)
-    gain = jnp.concatenate([by_shard[:, :256].reshape(1, -1), by_shard[:, 256:].reshape(1, -1)], axis=1)
     half = 1000000.0 ** -(np.arange(HD // 2, dtype=np.float32) * np.float32(2.0 / HD))
     freq = jnp.asarray(np.concatenate([half, half])[None, :].astype(np.float32))
     vmem = pl.BlockSpec(memory_space=pltpu.VMEM)
@@ -436,8 +455,8 @@
             pltpu.VMEM((HD, T), jnp.bfloat16),
             pltpu.VMEM((8, HD), jnp.int32),
             pltpu.VMEM((T, HD), jnp.float32),
-            pltpu.SemaphoreType.DMA((9,)),
-            pltpu.SemaphoreType.DMA((9,)),
+            pltpu.SemaphoreType.DMA((14,)),
+            pltpu.SemaphoreType.DMA((14,)),
             pltpu.SemaphoreType.DMA((20,)),
             pltpu.SemaphoreType.DMA((20,)),
             pltpu.SemaphoreType.DMA((20,)),
@@ -449,7 +468,7 @@
         cost_estimate=pl.CostEstimate(flops=7 * 10**9, bytes_accessed=4 * 10**6, transcendentals=10**7),
     )(
         hidden,
-        gain,
+        norm_gain,
         query_weight,
         key_weight,
         value_weight,

time: 72.6 us -> 68 us (0.937)
  Pallas kernels: 67.3 us -> 63.7 us
  local copies, waits for them, and re-layouts: 4.29 us -> 3.4 us
    pallas_call x1, Pallas kernels: 67.3 us -> 63.7 us  [shards(): pl.pallas_call(kernel, out_shape=(jax.ShapeDtypeStruct((T, G * HD), jnp.b...]
    reshape x2 -> x0, local copies, waits for them, and re-layouts: 0.86 us -> none  [the longest x1 0.78 us: shards(): by_shard = norm_gain.reshape(TP, F)]
where the time goes in v3:
time: 68 us; the launch traced here: 67.9 us
  Pallas kernels  63.7 us (94%)
  local copies, waits for them, and re-layouts  3.4 us (5%)
  between operations  0.79 us (1%)
    pallas_call x1, Pallas kernels, shards(): pl.pallas_call(kernel, out_shape=(jax.ShapeDtypeStruct((T, G * HD), jnp.b...  63.7 us
    unnamed x22, local copies, waits for them, and re-layouts  3.4 us

profile of v3, /device:TPU:24, one launch (start us, length us, event | category | flops | bytes accessed | tf_op | source)
XLA Modules:
  0.0 67.9 jit_solution(11935676786351581324)
XLA Ops:
  0.6 0.0 copy-start
  0.6 0.0 copy-start.1
  0.7 0.0 copy-start.2
  0.7 0.0 copy-start.3
  0.7 0.0 copy-start.4
  0.7 0.0 copy-start.5
  0.7 0.0 copy-start.6
  0.7 0.0 copy-start.7
  0.7 0.0 copy-start.8
  0.7 1.3 %copy.13.hid_ref = bf16[512,320]{1,0:T(8,128)(2,1)S(1)} copy(bf16[512,320]{0,1:T(8,128)(2,1)} %param.10) | data formatting | bytes 655360 | tf_op args[0]
  2.0 0.0 copy-done
  2.0 0.0 copy-done.1
  2.0 0.0 copy-done.2
  2.0 0.0 copy-done.3
  2.0 0.0 copy-done.4
  2.0 0.0 copy-done.5
  2.0 0.0 copy-done.6
  2.1 0.0 copy-done.7
  2.1 0.0 copy-done.8
  2.1 63.7 %shard_map.121 = (bf16[512,512]{1,0:T(8,128)(2,1)S(1)}, bf16[4,1,128,128]{3,2,1,0:T(8,128)(2,1)S(1)}, bf16[4,1,128,128]{3,2,1,0:T(8,128)(2,1)S(1)}) custom-call(bf16[512,320]{1,0:T(8,128)(2,1)S(1)} %copy.13.hid_ref, f32[2560]{0:T(1024)S(1)} %copy-done.3, f32[160,512]{1,0:T(8,128)S(1)} %copy-done, f32[160,128]{1,0:T(8,128)S(1)} %copy-done.1, ...), custom_call_target="tpu_custom_call" | custom-call | flops 7000000000 | bytes 4000000 | tf_op jit(solution)/shard_map/pallas_call | solution.py:435
  65.8 0.8 %copy.17 = bf16[512,512]{1,0:T(8,128)(2,1)} copy(bf16[512,512]{1,0:T(8,128)(2,1)S(1)} %get-tuple-element.6) | data formatting | bytes 1048576
  66.6 0.7 copy.18
  67.2 0.7 copy.19
Async XLA Ops:
  0.6 1.4 %copy-start = (f32[160,512]{1,0:T(8,128)S(1)}, f32[160,512]{1,0:T(8,128)}, u32[]{:S(2)}) copy-start(f32[160,512]{1,0:T(8,128)} %wq_ref.1) | copy-start | bytes 983044
  0.6 1.4 %copy-start.1 = (f32[160,128]{1,0:T(8,128)S(1)}, f32[160,128]{1,0:T(8,128)}, u32[]{:S(2)}) copy-start(f32[160,128]{1,0:T(8,128)} %wk_ref.1) | copy-start | bytes 245764
  0.7 1.4 %copy-start.2 = (f32[160,128]{1,0:T(8,128)S(1)}, f32[160,128]{1,0:T(8,128)}, u32[]{:S(2)}) copy-start(f32[160,128]{1,0:T(8,128)} %wv_ref.1) | copy-start | bytes 245764
  0.7 1.4 %copy-start.3 = (f32[2560]{0:T(1024)S(1)}, f32[2560]{0:T(1024)}, u32[]{:S(2)}) copy-start(f32[2560]{0:T(1024)} %gain_1d.1) | copy-start | bytes 30724
  0.7 1.4 %copy-start.4 = (f32[128]{0:T(128)S(1)}, f32[128]{0:T(128)}, u32[]{:S(2)}) copy-start(f32[128]{0:T(128)} %param.15) | copy-start | bytes 1540
  0.7 1.4 %copy-start.5 = (f32[128]{0:T(128)S(1)}, f32[128]{0:T(128)}, u32[]{:S(2)}) copy-start(f32[128]{0:T(128)} %param.16) | copy-start | bytes 1540
  0.7 1.4 %copy-start.6 = (s32[8]{0:T(128)S(1)}, s32[8]{0:T(128)}, u32[]{:S(2)}) copy-start(s32[8]{0:T(128)} %len_ref.1) | copy-start | bytes 100
  0.7 1.4 %copy-start.7 = (s32[64]{0:T(128)S(1)}, s32[64]{0:T(128)}, u32[]{:S(2)}) copy-start(s32[64]{0:T(128)} %pt_ref.1) | copy-start | bytes 772
  0.7 1.4 %copy-start.8 = (f32[1,128]{1,0:T(1,128)S(1)}, f32[1,128]{1,0:T(1,128)}, u32[]{:S(2)}) copy-start(f32[1,128]{1,0:T(1,128)} %constant.2.clone.freq_ref) | copy-start | bytes 1540

commit v4 on v3

--- a/solution.py
+++ b/solution.py
@@ -149,13 +149,6 @@
         4: ((1, 8, xm),),
     }
 
-    def seq_begin(g):
-        rank = seq_rank(0, 0, 0)
-        g.go(rank, None, 0, yhp)
-        g.go(rank, None, 1, xp)
-        g.go(rank, None, 3, xm)
-        g.go(rank, None, 10, sib)
-
     def seq_pass(g, role):
         dx, dy, half = seq_roles[role]
         rank = seq_rank(dx, dy, 0)
@@ -190,6 +183,34 @@
 
     def tp_begin(name, piece, peer):
         gh.go(t, piece, tp_index[name] + piece, peer)
+
+    kv_roles = {"xm": (3, 0), "xp": (1, 0), "y": (0, 1), "x2": (2, 0), "xmy": (3, 1), "xpy": (1, 1), "x2y": (2, 1)}
+    kv_index = {name: i for i, name in enumerate(kv_roles)}
+    kv_forward = {
+        ("xm", 0): (("x2", xp),),
+        ("xp", 1): (("x2", xm),),
+        ("y", 0): (("xmy", xp), ("xpy", xm)),
+        ("y", 1): (("xmy", xp), ("xpy", xm)),
+        ("x2", 0): (("x2y", yhp),),
+        ("x2", 1): (("x2y", yhp),),
+    }
+
+    def kv_begin():
+        for name, piece, peer in (("xm", 0, xp), ("xp", 1, xm), ("y", 0, yhp), ("y", 1, yhp), ("xm", 1, xp), ("xp", 0, xm)):
+            gk.go(s, piece, 2 * kv_index[name] + piece, peer)
+        gk.go(s, None, 21, sib)
+
+    def kv_pass(name, piece):
+        rank = seq_rank(*kv_roles[name], 0)
+        gk.wait(rank, piece, 2 * kv_index[name] + piece)
+        for to, peer in kv_forward.get((name, piece), ()):
+            gk.go(rank, piece, 2 * kv_index[to] + piece, peer)
+
+    def kv_share(name):
+        gk.go(seq_rank(*kv_roles[name], 0), None, 14 + kv_index[name], sib)
+
+    def kv_sib(name):
+        gk.wait(seq_rank(*kv_roles[name], 1), None, 14 + kv_index[name])
 
     gh = Gather(h_region, h_send, h_recv)
     gw = Gather(w_region, w_send, w_recv)
@@ -330,7 +351,7 @@
     for i in range(T // PAGE):
         kv[s * 8 + i] = keys[PAGE * i : PAGE * i + PAGE, :]
         kv[s * 8 + per + i] = vt[:, PAGE * i : PAGE * i + PAGE]
-    seq_begin(gk)
+    kv_begin()
 
     for pair in range(G // 2):
         qp = project(256 * pair, 256 * pair + 256)
@@ -392,26 +413,30 @@
         lax.fori_loop(0, len(offsets), one, 0)
 
     attend(s, True)
-    seq_pass(gk, 0)
-    seq_pass(gk, 1)
-    seq_pass(gk, 3)
-    seq_sib(gk, None)
+    for name, piece in (("xm", 0), ("xp", 1), ("xm", 1), ("xp", 0), ("y", 0), ("y", 1)):
+        kv_pass(name, piece)
+    for name in ("y", "xm", "xp"):
+        kv_share(name)
+    gk.wait(seq_rank(0, 0, 1), None, 21)
     attend_all([(0, 0, 1), (0, 1, 0)])
-    seq_pass(gk, 2)
-    seq_pass(gk, 4)
-    for role in (0, 1, 3):
-        seq_sib(gk, role)
-    attend_all([(3, 0, 0), (1, 0, 0), (0, 1, 1)])
-    for role in (5, 7):
-        seq_pass(gk, role)
-    attend_all([(3, 0, 1), (1, 0, 1), (3, 1, 0), (1, 1, 0), (2, 0, 0)])
-    for role in (6, 8):
-        seq_pass(gk, role)
-    for role in (2, 4, 5, 7):
-        seq_sib(gk, role)
-    attend_all([(3, 1, 1), (1, 1, 1), (2, 0, 1), (2, 1, 0)])
-    for role in (6, 8):
-        seq_sib(gk, role)
+    kv_pass("x2", 0)
+    kv_pass("x2", 1)
+    kv_share("x2")
+    attend_all([(3, 0, 0), (1, 0, 0)])
+    for name, piece in (("xmy", 0), ("xpy", 0), ("xmy", 1), ("xpy", 1)):
+        kv_pass(name, piece)
+    kv_share("xmy")
+    kv_share("xpy")
+    for name in ("y", "xm", "xp"):
+        kv_sib(name)
+    attend_all([(0, 1, 1), (3, 0, 1), (1, 0, 1), (3, 1, 0), (1, 1, 0)])
+    kv_pass("x2y", 0)
+    kv_pass("x2y", 1)
+    kv_share("x2y")
+    for name in ("x2", "xmy", "xpy"):
+        kv_sib(name)
+    attend_all([(2, 0, 0), (3, 1, 1), (1, 1, 1), (2, 0, 1), (2, 1, 0)])
+    kv_sib("x2y")
     attend_all([(2, 1, 1)])
 
     for h in range(G):
@@ -459,8 +484,8 @@
             pltpu.SemaphoreType.DMA((14,)),
             pltpu.SemaphoreType.DMA((20,)),
             pltpu.SemaphoreType.DMA((20,)),
-            pltpu.SemaphoreType.DMA((20,)),
-            pltpu.SemaphoreType.DMA((20,)),
+            pltpu.SemaphoreType.DMA((22,)),
+            pltpu.SemaphoreType.DMA((22,)),
         ],
         compiler_params=pltpu.CompilerParams(
             collective_id=0, has_side_effects=True, vmem_limit_bytes=48 * 1024 * 1024

time: 68 us -> 66 us (0.971)
  Pallas kernels: 63.7 us -> 61.7 us
    pallas_call x1, Pallas kernels: 63.7 us -> 61.7 us  [shards(): pl.pallas_call(kernel, out_shape=(jax.ShapeDtypeStruct((T, G * HD), jnp.b...]
where the time goes in v4:
time: 66 us; the launch traced here: 65.8 us
  Pallas kernels  61.7 us (93%)
  local copies, waits for them, and re-layouts  3.4 us (5%)
  between operations  0.79 us (1%)
    pallas_call x1, Pallas kernels, shards(): pl.pallas_call(kernel, out_shape=(jax.ShapeDtypeStruct((T, G * HD), jnp.b...  61.7 us
    unnamed x22, local copies, waits for them, and re-layouts  3.4 us

profile of v4, /device:TPU:24, one launch (start us, length us, event | category | flops | bytes accessed | tf_op | source)
XLA Modules:
  0.0 65.8 jit_solution(1869709884651705463)
XLA Ops:
  0.6 0.0 copy-start
  0.6 0.0 copy-start.1
  0.7 0.0 copy-start.2
  0.7 0.0 copy-start.3
  0.7 0.0 copy-start.4
  0.7 0.0 copy-start.5
  0.7 0.0 copy-start.6
  0.7 0.0 copy-start.7
  0.7 0.0 copy-start.8
  0.7 1.3 %copy.13.hid_ref = bf16[512,320]{1,0:T(8,128)(2,1)S(1)} copy(bf16[512,320]{0,1:T(8,128)(2,1)} %param.10) | data formatting | bytes 655360 | tf_op args[0]
  2.0 0.0 copy-done
  2.0 0.0 copy-done.1
  2.0 0.0 copy-done.2
  2.0 0.0 copy-done.3
  2.0 0.0 copy-done.4
  2.0 0.0 copy-done.5
  2.0 0.0 copy-done.6
  2.1 0.0 copy-done.7
  2.1 0.0 copy-done.8
  2.1 61.7 %shard_map.121 = (bf16[512,512]{1,0:T(8,128)(2,1)S(1)}, bf16[4,1,128,128]{3,2,1,0:T(8,128)(2,1)S(1)}, bf16[4,1,128,128]{3,2,1,0:T(8,128)(2,1)S(1)}) custom-call(bf16[512,320]{1,0:T(8,128)(2,1)S(1)} %copy.13.hid_ref, f32[2560]{0:T(1024)S(1)} %copy-done.3, f32[160,512]{1,0:T(8,128)S(1)} %copy-done, f32[160,128]{1,0:T(8,128)S(1)} %copy-done.1, ...), custom_call_target="tpu_custom_call" | custom-call | flops 7000000000 | bytes 4000000 | tf_op jit(solution)/shard_map/pallas_call | solution.py:460
  63.7 0.8 %copy.17 = bf16[512,512]{1,0:T(8,128)(2,1)} copy(bf16[512,512]{1,0:T(8,128)(2,1)S(1)} %get-tuple-element.6) | data formatting | bytes 1048576
  64.5 0.7 copy.18
  65.2 0.7 copy.19
Async XLA Ops:
  0.6 1.4 %copy-start = (f32[160,512]{1,0:T(8,128)S(1)}, f32[160,512]{1,0:T(8,128)}, u32[]{:S(2)}) copy-start(f32[160,512]{1,0:T(8,128)} %wq_ref.1) | copy-start | bytes 983044
  0.6 1.4 %copy-start.1 = (f32[160,128]{1,0:T(8,128)S(1)}, f32[160,128]{1,0:T(8,128)}, u32[]{:S(2)}) copy-start(f32[160,128]{1,0:T(8,128)} %wk_ref.1) | copy-start | bytes 245764
  0.7 1.4 %copy-start.2 = (f32[160,128]{1,0:T(8,128)S(1)}, f32[160,128]{1,0:T(8,128)}, u32[]{:S(2)}) copy-start(f32[160,128]{1,0:T(8,128)} %wv_ref.1) | copy-start | bytes 245764
  0.7 1.4 %copy-start.3 = (f32[2560]{0:T(1024)S(1)}, f32[2560]{0:T(1024)}, u32[]{:S(2)}) copy-start(f32[2560]{0:T(1024)} %gain_1d.1) | copy-start | bytes 30724
  0.7 1.4 %copy-start.4 = (f32[128]{0:T(128)S(1)}, f32[128]{0:T(128)}, u32[]{:S(2)}) copy-start(f32[128]{0:T(128)} %param.15) | copy-start | bytes 1540
  0.7 1.4 %copy-start.5 = (f32[128]{0:T(128)S(1)}, f32[128]{0:T(128)}, u32[]{:S(2)}) copy-start(f32[128]{0:T(128)} %param.16) | copy-start | bytes 1540
  0.7 1.4 %copy-start.6 = (s32[8]{0:T(128)S(1)}, s32[8]{0:T(128)}, u32[]{:S(2)}) copy-start(s32[8]{0:T(128)} %len_ref.1) | copy-start | bytes 100
  0.7 1.4 %copy-start.7 = (s32[64]{0:T(128)S(1)}, s32[64]{0:T(128)}, u32[]{:S(2)}) copy-start(s32[64]{0:T(128)} %pt_ref.1) | copy-start | bytes 772
  0.7 1.4 %copy-start.8 = (f32[1,128]{1,0:T(1,128)S(1)}, f32[1,128]{1,0:T(1,128)}, u32[]{:S(2)}) copy-start(f32[1,128]{1,0:T(1,128)} %constant.2.clone.freq_ref) | copy-start | bytes 1540

commit v5 on v4

--- a/solution.py
+++ b/solution.py
@@ -55,6 +55,7 @@
     other,
     bounds,
     ssq,
+    hb,
     h_send,
     h_recv,
     w_send,
@@ -216,13 +217,13 @@
     gw = Gather(w_region, w_send, w_recv)
     gk = Gather(kv_region, kv_send, kv_recv)
 
-    tp_begin("zm", 0, zp)
-    tp_begin("zp", 1, zm)
+    gw.go(s, None, 0, yhp)
     tp_begin("y", 0, ylp)
-    gw.go(s, None, 0, yhp)
     tp_begin("y", 1, ylp)
     gw.go(s, None, 1, xp)
     gw.go(s, None, 3, xm)
+    tp_begin("zm", 0, zp)
+    tp_begin("zp", 1, zm)
     tp_begin("zm", 1, zp)
     tp_begin("zp", 0, zm)
     gw.go(s, None, 10, sib)
@@ -275,41 +276,30 @@
         ssq[...] += v[:, 0:HD] + v[:, HD:]
 
     add_squares(t)
-    for name, piece in (("zm", 0), ("zp", 1)):
-        tp_pass(name, piece)
     seq_pass(gw, 1)
     seq_pass(gw, 3)
-    for name, piece in (("zm", 1), ("zp", 0), ("y", 0)):
+    for name, piece in (("zm", 0), ("zp", 0), ("zp", 1), ("zm", 1)):
         tp_pass(name, piece)
     seq_pass(gw, 0)
+    tp_pass("y", 0)
     tp_pass("y", 1)
+    seq_pass(gw, 5)
     tp_pass("z2", 0)
-    seq_pass(gw, 5)
+    seq_pass(gw, 7)
     tp_pass("z2", 1)
-    seq_pass(gw, 7)
+    seq_pass(gw, 2)
+    seq_pass(gw, 4)
     for dz, dy in ((0, 1), (1, 0), (3, 0), (2, 0)):
         add_squares(tp_rank(dz, dy))
-    seq_pass(gw, 2)
-    seq_pass(gw, 4)
     for name, piece in (("zmy", 0), ("zpy", 0), ("zmy", 1), ("zpy", 1)):
         tp_pass(name, piece)
     seq_pass(gw, 6)
     seq_pass(gw, 8)
     add_squares(tp_rank(3, 1))
     add_squares(tp_rank(1, 1))
-    tp_pass("z2y", 0)
-    tp_pass("z2y", 1)
-    add_squares(tp_rank(2, 1))
-    seq_sib(gw, None)
-    for role in range(9):
-        seq_sib(gw, role)
-
-    gain_row = gain_1d[...].reshape(1, D)
-    gain_ref = [gain_row[:, F * i : F * i + 256] for i in range(TP)]
-    gain_last = jnp.concatenate([gain_row[:, F * i + 256 : F * i + F] for i in range(TP)], axis=1)
-
     half_lane = lax.broadcasted_iota(jnp.int32, (128, 128), 1) < 64
-    for pair in range(TP // 2):
+
+    def unpack(pair):
         for col in range(2):
             lanes = slice(128 * col, 128 * col + 128)
             a = hall[2 * pair, T : T + 128, lanes].astype(jnp.float32)
@@ -319,14 +309,30 @@
             for q, v in ((2 * col, low), (2 * col + 1, high)):
                 where = slice(128 * q, 128 * q + 128)
                 ssq[where, :] += v * v
-                hn[where, 2048 + 128 * pair : 2176 + 128 * pair] = v.astype(jnp.bfloat16)
+                hb[pair, where, :] = v.astype(jnp.bfloat16)
+
+    corner = tp_rank(2, 1)
+    for i in range(1, TP // 2):
+        unpack((corner // 2 + i) % (TP // 2))
+    gain_row = gain_1d[...].reshape(1, D)
+    gain_ref = [gain_row[:, F * i : F * i + 256] for i in range(TP)]
+    gain_last = jnp.concatenate([gain_row[:, F * i + 256 : F * i + F] for i in range(TP)], axis=1)
+    seq_sib(gw, None)
+    for role in range(9):
+        seq_sib(gw, role)
+    tp_pass("z2y", 0)
+    tp_pass("z2y", 1)
+    add_squares(corner)
+    unpack(corner // 2)
 
     scale = lax.rsqrt(jnp.sum(ssq[...], axis=1, keepdims=True) * (1.0 / D) + EPS)
     for i in range(TP):
         v = hall[i, 0:T, :].astype(jnp.float32) * scale
         hn[:, 256 * i : 256 * i + 256] = (v * gain_ref[i]).astype(jnp.bfloat16)
-    v = hn[:, 2048:].astype(jnp.float32) * scale
-    hn[:, 2048:] = (v * gain_last).astype(jnp.bfloat16)
+    for i in range(TP // 2):
+        v = hb[i].astype(jnp.float32) * scale
+        at = 2048 + HD * i
+        hn[:, at : at + HD] = (v * gain_last[:, HD * i : HD * i + HD]).astype(jnp.bfloat16)
 
     def project(lo, hi):
         total = None
@@ -361,18 +367,41 @@
 
     ones = jnp.where(lax.broadcasted_iota(jnp.int32, (VE - HD, T), 0) == 0, 1.0, 0.0).astype(jnp.bfloat16)
 
-    def attend(rank, diagonal):
+    def blocks(rank):
         keys = jnp.concatenate([kv[rank * 8 + i] for i in range(per)], axis=0)
         vals = jnp.concatenate([kv[rank * 8 + per + i] for i in range(per)], axis=1)
-        vals = jnp.concatenate([vals, ones], axis=0)
-        if not diagonal:
-            key_slot = rank * T + lax.broadcasted_iota(jnp.int32, (T, HD), 0)
-            member = (key_slot >= bounds[0:1, :]) & (key_slot < bounds[1:2, :])
-            keys = jnp.concatenate([keys, jnp.where(member, 1.0, 0.0).astype(jnp.bfloat16)], axis=1)
+        return keys, jnp.concatenate([vals, ones], axis=0)
+
+    def attend_own():
+        keys, vals = blocks(s)
+        wide = T // 2
+        parts = [(h, half) for h in range(G) for half in range(2)]
+
+        def score(h, half):
+            queries = qt[h][:, wide * half : wide * half + wide]
+            return jnp.dot(keys[: wide * (half + 1), :], queries, preferred_element_type=jnp.float32)
+
+        ahead = score(*parts[0])
+        for i, (h, half) in enumerate(parts):
+            scores, count, at = ahead, wide * (half + 1), slice(wide * half, wide * half + wide)
+            if i + 1 < len(parts):
+                ahead = score(*parts[i + 1])
+            key_slot = lax.broadcasted_iota(jnp.int32, (count, wide), 0)
+            query_slot = wide * half + lax.broadcasted_iota(jnp.int32, (count, wide), 1)
+            allowed = (key_slot >= startr[0:1, at] - s * T) & (key_slot <= query_slot)
+            scores = jnp.where(allowed, scores, EXCLUDED)
+            top = jnp.max(scores, axis=0, keepdims=True)
+            probs = jnp.exp2((scores - top) * SCALE).astype(jnp.bfloat16)
+            acc[h, :, at] = jnp.dot(vals[:, :count], probs, preferred_element_type=jnp.float32)
+            mx[h, :, at] = top
+
+    def attend(rank):
+        keys, vals = blocks(rank)
+        key_slot = rank * T + lax.broadcasted_iota(jnp.int32, (T, HD), 0)
+        member = (key_slot >= bounds[0:1, :]) & (key_slot < bounds[1:2, :])
+        keys = jnp.concatenate([keys, jnp.where(member, 1.0, 0.0).astype(jnp.bfloat16)], axis=1)
 
         def score(h):
-            if diagonal:
-                return jnp.dot(keys, qt[h], preferred_element_type=jnp.float32)
             queries = jnp.concatenate([qt[h], other[...]], axis=0)
             return jnp.dot(keys, queries, preferred_element_type=jnp.float32)
 
@@ -381,21 +410,11 @@
             scores = ahead
             if h + 1 < G:
                 ahead = score(h + 1)
-            if diagonal:
-                key_slot = rank * T + lax.broadcasted_iota(jnp.int32, (T, T), 0)
-                query_slot = rank * T + lax.broadcasted_iota(jnp.int32, (T, T), 1)
-                allowed = (key_slot >= startr[0:1, :]) & (key_slot <= query_slot)
-                scores = jnp.where(allowed, scores, EXCLUDED)
-            top = jnp.max(scores, axis=0, keepdims=True)
-            if not diagonal:
-                old = mx[h]
-                top = jnp.maximum(old, top)
+            old = mx[h]
+            top = jnp.maximum(old, jnp.max(scores, axis=0, keepdims=True))
             probs = jnp.exp2((scores - top) * SCALE).astype(jnp.bfloat16)
             sums = jnp.dot(vals, probs, preferred_element_type=jnp.float32)
-            if diagonal:
-                acc[h] = sums
-            else:
-                acc[h] = acc[h] * jnp.exp2((old - top) * SCALE) + sums
+            acc[h] = acc[h] * jnp.exp2((old - top) * SCALE) + sums
             mx[h] = top
 
     def attend_all(offsets):
@@ -406,13 +425,13 @@
 
             @pl.when((rank < s) & (rank + 8 >= s))
             def _():
-                attend(rank, False)
+                attend(rank)
 
             return carry
 
         lax.fori_loop(0, len(offsets), one, 0)
 
-    attend(s, True)
+    attend_own()
     for name, piece in (("xm", 0), ("xp", 1), ("xm", 1), ("xp", 0), ("y", 0), ("y", 1)):
         kv_pass(name, piece)
     for name in ("y", "xm", "xp"):
@@ -440,7 +459,7 @@
     attend_all([(2, 1, 1)])
 
     for h in range(G):
-        o = acc[h, 0:HD, :] / acc[h, HD : HD + 1, :]
+        o = acc[h, 0:HD, :] * (1.0 / acc[h, HD : HD + 1, :])
         out_ref[:, HD * h : HD * h + HD] = o.T.astype(jnp.bfloat16)
 
     for i in range(per):
@@ -480,6 +499,7 @@
             pltpu.VMEM((HD, T), jnp.bfloat16),
             pltpu.VMEM((8, HD), jnp.int32),
             pltpu.VMEM((T, HD), jnp.float32),
+            pltpu.VMEM((TP // 2, T, HD), jnp.bfloat16),
             pltpu.SemaphoreType.DMA((14,)),
             pltpu.SemaphoreType.DMA((14,)),
             pltpu.SemaphoreType.DMA((20,)),

time: 66 us -> 64.1 us (0.971)
  Pallas kernels: 61.7 us -> 59.8 us
    pallas_call x1, Pallas kernels: 61.7 us -> 59.8 us  [shards(): pl.pallas_call(kernel, out_shape=(jax.ShapeDtypeStruct((T, G * HD), jnp.b...]
where the time goes in v5:
time: 64.1 us; the launch traced here: 64 us
  Pallas kernels  59.8 us (93%)
  local copies, waits for them, and re-layouts  3.4 us (5%)
  between operations  0.79 us (1%)
    pallas_call x1, Pallas kernels, shards(): pl.pallas_call(kernel, out_shape=(jax.ShapeDtypeStruct((T, G * HD), jnp.b...  59.8 us
    unnamed x22, local copies, waits for them, and re-layouts  3.4 us

profile of v5, /device:TPU:24, one launch (start us, length us, event | category | flops | bytes accessed | tf_op | source)
XLA Modules:
  0.0 64.0 jit_solution(14007615516910129586)
XLA Ops:
  0.6 0.0 copy-start
  0.6 0.0 copy-start.1
  0.7 0.0 copy-start.2
  0.7 0.0 copy-start.3
  0.7 0.0 copy-start.4
  0.7 0.0 copy-start.5
  0.7 0.0 copy-start.6
  0.7 0.0 copy-start.7
  0.7 0.0 copy-start.8
  0.7 1.3 %copy.13.hid_ref = bf16[512,320]{1,0:T(8,128)(2,1)S(1)} copy(bf16[512,320]{0,1:T(8,128)(2,1)} %param.10) | data formatting | bytes 655360 | tf_op args[0]
  2.0 0.0 copy-done
  2.0 0.0 copy-done.1
  2.0 0.0 copy-done.2
  2.0 0.0 copy-done.3
  2.0 0.0 copy-done.4
  2.0 0.0 copy-done.5
  2.0 0.0 copy-done.6
  2.1 0.0 copy-done.7
  2.1 0.0 copy-done.8
  2.1 59.8 %shard_map.121 = (bf16[512,512]{1,0:T(8,128)(2,1)S(1)}, bf16[4,1,128,128]{3,2,1,0:T(8,128)(2,1)S(1)}, bf16[4,1,128,128]{3,2,1,0:T(8,128)(2,1)S(1)}) custom-call(bf16[512,320]{1,0:T(8,128)(2,1)S(1)} %copy.13.hid_ref, f32[2560]{0:T(1024)S(1)} %copy-done.3, f32[160,512]{1,0:T(8,128)S(1)} %copy-done, f32[160,128]{1,0:T(8,128)S(1)} %copy-done.1, ...), custom_call_target="tpu_custom_call" | custom-call | flops 7000000000 | bytes 4000000 | tf_op jit(solution)/shard_map/pallas_call | solution.py:479
  61.9 0.8 %copy.17 = bf16[512,512]{1,0:T(8,128)(2,1)} copy(bf16[512,512]{1,0:T(8,128)(2,1)S(1)} %get-tuple-element.6) | data formatting | bytes 1048576
  62.7 0.7 %copy.18 = bf16[4,1,128,128]{3,2,1,0:T(8,128)(2,1)} copy(bf16[4,1,128,128]{3,2,1,0:T(8,128)(2,1)S(1)} %get-tuple-element.7) | data formatting | bytes 262144
  63.3 0.7 %copy.19 = bf16[4,1,128,128]{3,2,1,0:T(8,128)(2,1)} copy(bf16[4,1,128,128]{3,2,1,0:T(8,128)(2,1)S(1)} %get-tuple-element.8) | data formatting | bytes 262144
Async XLA Ops:
  0.6 1.4 %copy-start = (f32[160,512]{1,0:T(8,128)S(1)}, f32[160,512]{1,0:T(8,128)}, u32[]{:S(2)}) copy-start(f32[160,512]{1,0:T(8,128)} %wq_ref.1) | copy-start | bytes 983044
  0.6 1.4 %copy-start.1 = (f32[160,128]{1,0:T(8,128)S(1)}, f32[160,128]{1,0:T(8,128)}, u32[]{:S(2)}) copy-start(f32[160,128]{1,0:T(8,128)} %wk_ref.1) | copy-start | bytes 245764
  0.7 1.4 %copy-start.2 = (f32[160,128]{1,0:T(8,128)S(1)}, f32[160,128]{1,0:T(8,128)}, u32[]{:S(2)}) copy-start(f32[160,128]{1,0:T(8,128)} %wv_ref.1) | copy-start | bytes 245764
  0.7 1.4 %copy-start.3 = (f32[2560]{0:T(1024)S(1)}, f32[2560]{0:T(1024)}, u32[]{:S(2)}) copy-start(f32[2560]{0:T(1024)} %gain_1d.1) | copy-start | bytes 30724
  0.7 1.4 %copy-start.4 = (f32[128]{0:T(128)S(1)}, f32[128]{0:T(128)}, u32[]{:S(2)}) copy-start(f32[128]{0:T(128)} %param.15) | copy-start | bytes 1540
  0.7 1.4 %copy-start.5 = (f32[128]{0:T(128)S(1)}, f32[128]{0:T(128)}, u32[]{:S(2)}) copy-start(f32[128]{0:T(128)} %param.16) | copy-start | bytes 1540
  0.7 1.4 %copy-start.6 = (s32[8]{0:T(128)S(1)}, s32[8]{0:T(128)}, u32[]{:S(2)}) copy-start(s32[8]{0:T(128)} %len_ref.1) | copy-start | bytes 100
  0.7 1.4 %copy-start.7 = (s32[64]{0:T(128)S(1)}, s32[64]{0:T(128)}, u32[]{:S(2)}) copy-start(s32[64]{0:T(128)} %pt_ref.1) | copy-start | bytes 772
  0.7 1.4 %copy-start.8 = (f32[1,128]{1,0:T(1,128)S(1)}, f32[1,128]{1,0:T(1,128)}, u32[]{:S(2)}) copy-start(f32[1,128]{1,0:T(1,128)} %constant.2.clone.freq_ref) | copy-start | bytes 1540

commit v6 on v5

--- a/solution.py
+++ b/solution.py
@@ -197,7 +197,7 @@
     }
 
     def kv_begin():
-        for name, piece, peer in (("xm", 0, xp), ("xp", 1, xm), ("y", 0, yhp), ("y", 1, yhp), ("xm", 1, xp), ("xp", 0, xm)):
+        for name, piece, peer in (("y", 0, yhp), ("y", 1, yhp), ("xm", 0, xp), ("xp", 1, xm), ("xm", 1, xp), ("xp", 0, xm)):
             gk.go(s, piece, 2 * kv_index[name] + piece, peer)
         gk.go(s, None, 21, sib)
 

time: 64.1 us -> 64.1 us (level)
  no operation moved by 1% of the time
where the time goes in v6:
time: 64.1 us; the launch traced here: 64 us
  Pallas kernels  59.8 us (93%)
  local copies, waits for them, and re-layouts  3.4 us (5%)
  between operations  0.79 us (1%)
    pallas_call x1, Pallas kernels, shards(): pl.pallas_call(kernel, out_shape=(jax.ShapeDtypeStruct((T, G * HD), jnp.b...  59.8 us
    unnamed x22, local copies, waits for them, and re-layouts  3.4 us

profile of v6, /device:TPU:24, one launch (start us, length us, event | category | flops | bytes accessed | tf_op | source)
XLA Modules:
  0.0 64.0 jit_solution(2120821365244139407)
XLA Ops:
  0.6 0.0 copy-start
  0.6 0.0 copy-start.1
  0.7 0.0 copy-start.2
  0.7 0.0 copy-start.3
  0.7 0.0 copy-start.4
  0.7 0.0 copy-start.5
  0.7 0.0 copy-start.6
  0.7 0.0 copy-start.7
  0.7 0.0 copy-start.8
  0.7 1.3 %copy.13.hid_ref = bf16[512,320]{1,0:T(8,128)(2,1)S(1)} copy(bf16[512,320]{0,1:T(8,128)(2,1)} %param.10) | data formatting | bytes 655360 | tf_op args[0]
  2.0 0.0 copy-done
  2.0 0.0 copy-done.1
  2.0 0.0 copy-done.2
  2.0 0.0 copy-done.3
  2.0 0.0 copy-done.4
  2.0 0.0 copy-done.5
  2.0 0.0 copy-done.6
  2.1 0.0 copy-done.7
  2.1 0.0 copy-done.8
  2.1 59.8 %shard_map.121 = (bf16[512,512]{1,0:T(8,128)(2,1)S(1)}, bf16[4,1,128,128]{3,2,1,0:T(8,128)(2,1)S(1)}, bf16[4,1,128,128]{3,2,1,0:T(8,128)(2,1)S(1)}) custom-call(bf16[512,320]{1,0:T(8,128)(2,1)S(1)} %copy.13.hid_ref, f32[2560]{0:T(1024)S(1)} %copy-done.3, f32[160,512]{1,0:T(8,128)S(1)} %copy-done, f32[160,128]{1,0:T(8,128)S(1)} %copy-done.1, ...), custom_call_target="tpu_custom_call" | custom-call | flops 7000000000 | bytes 4000000 | tf_op jit(solution)/shard_map/pallas_call | solution.py:479
  61.9 0.8 %copy.17 = bf16[512,512]{1,0:T(8,128)(2,1)} copy(bf16[512,512]{1,0:T(8,128)(2,1)S(1)} %get-tuple-element.6) | data formatting | bytes 1048576
  62.7 0.7 %copy.18 = bf16[4,1,128,128]{3,2,1,0:T(8,128)(2,1)} copy(bf16[4,1,128,128]{3,2,1,0:T(8,128)(2,1)S(1)} %get-tuple-element.7) | data formatting | bytes 262144
  63.3 0.7 %copy.19 = bf16[4,1,128,128]{3,2,1,0:T(8,128)(2,1)} copy(bf16[4,1,128,128]{3,2,1,0:T(8,128)(2,1)S(1)} %get-tuple-element.8) | data formatting | bytes 262144
Async XLA Ops:
  0.6 1.4 %copy-start = (f32[160,512]{1,0:T(8,128)S(1)}, f32[160,512]{1,0:T(8,128)}, u32[]{:S(2)}) copy-start(f32[160,512]{1,0:T(8,128)} %wq_ref.1) | copy-start | bytes 983044
  0.6 1.4 %copy-start.1 = (f32[160,128]{1,0:T(8,128)S(1)}, f32[160,128]{1,0:T(8,128)}, u32[]{:S(2)}) copy-start(f32[160,128]{1,0:T(8,128)} %wk_ref.1) | copy-start | bytes 245764
  0.7 1.4 %copy-start.2 = (f32[160,128]{1,0:T(8,128)S(1)}, f32[160,128]{1,0:T(8,128)}, u32[]{:S(2)}) copy-start(f32[160,128]{1,0:T(8,128)} %wv_ref.1) | copy-start | bytes 245764
  0.7 1.4 %copy-start.3 = (f32[2560]{0:T(1024)S(1)}, f32[2560]{0:T(1024)}, u32[]{:S(2)}) copy-start(f32[2560]{0:T(1024)} %gain_1d.1) | copy-start | bytes 30724
  0.7 1.4 %copy-start.4 = (f32[128]{0:T(128)S(1)}, f32[128]{0:T(128)}, u32[]{:S(2)}) copy-start(f32[128]{0:T(128)} %param.15) | copy-start | bytes 1540
  0.7 1.4 %copy-start.5 = (f32[128]{0:T(128)S(1)}, f32[128]{0:T(128)}, u32[]{:S(2)}) copy-start(f32[128]{0:T(128)} %param.16) | copy-start | bytes 1540
  0.7 1.4 %copy-start.6 = (s32[8]{0:T(128)S(1)}, s32[8]{0:T(128)}, u32[]{:S(2)}) copy-start(s32[8]{0:T(128)} %len_ref.1) | copy-start | bytes 100
  0.7 1.4 %copy-start.7 = (s32[64]{0:T(128)S(1)}, s32[64]{0:T(128)}, u32[]{:S(2)}) copy-start(s32[64]{0:T(128)} %pt_ref.1) | copy-start | bytes 772
  0.7 1.4 %copy-start.8 = (f32[1,128]{1,0:T(1,128)S(1)}, f32[1,128]{1,0:T(1,128)}, u32[]{:S(2)}) copy-start(f32[1,128]{1,0:T(1,128)} %constant.2.clone.freq_ref) | copy-start | bytes 1540
